TPU v7x, 256 devices: a whole 4x4x8 slice. The times are simulated.
256 devices in a mesh: ens: 16 (over x_lo, z), lat: 8 (over y, core), var: 2 (over x_hi).
Axes of the slice: x: 4 (x_hi: 2, x_lo: 2; x = x_hi * 2 + x_lo), y: 4, z: 8, core: 2. Of those that a mesh axis runs over, the one named last changes fastest.
Arguments:
- members: bfloat16 [16, 3, 12, 512, 1440], P('ens', None, 'var', 'lat'), may hold values from -6 to 6
- target: bfloat16 [3, 12, 512, 1440], P(None, 'var', 'lat'), may hold values from -6 to 6
- target_spectrum: bfloat16 [3, 12, 384, 2, 384], P(None, 'var', ('lat', 'ens')), may hold values from -5 to 5
- legendre: bfloat16 [384, 512, 384], P(('lat', 'ens')), may hold values from -0.25 to 0.25
- wavenum: int32 [384], replicated, may hold values from 0 to 383, each once
Outputs:
- member_grad: bfloat16 [16, 3, 12, 512, 1440], P('ens', None, 'var', 'lat')
- row_score: float32 [3, 12, 512], P(None, 'var', ('lat', 'ens'))
- spec_score: float32 [3, 12, 384], P(None, 'var', ('lat', 'ens'))
Inputs may be any that keep to these rules, and one draw needn't show every extreme that they name: Slot s holds zonal wavenumber wavenum[s], each of 0 to 383 once; slots holding a value above 360 carry no coefficients.
All inputs are finite; a program needn't handle non-finite values.
Results may differ from a plain program's by a relative error of at most 0.006.
Values may be sent and summed in bfloat16 or wider, within the bound.
A program may use at most 128 MiB of HBM per device.

v0:
```python
import math

import jax
import jax.numpy as jnp
from jax import lax
from jax.sharding import PartitionSpec as P

LMAX = 360


smooth_width = 0.25


def soft_abs(difference):
    return jnp.sqrt(difference * difference + smooth_width * smooth_width)


def fourier_table(wave_part, longitudes):
    points = jnp.arange(longitudes, dtype=jnp.int32)
    phase_index = points[:, None] * wave_part[None, :] % longitudes
    angles = phase_index.astype(jnp.float32) * (2.0 * math.pi / longitudes)
    factor = 1.0 / math.sqrt(longitudes)
    columns = jnp.stack([jnp.cos(angles) * factor, -jnp.sin(angles) * factor], axis=2)
    return columns.reshape(longitudes, 2 * wave_part.shape[0]).astype(jnp.bfloat16)


def spectral_masks(wave_part, degrees):
    degree = jnp.arange(degrees, dtype=jnp.int32)
    usable = (degree[None, :] >= wave_part[:, None]) & (degree[None, :] <= LMAX)
    double = jnp.where(wave_part == 0, 1.0, 2.0).astype(jnp.float32)
    weight = jnp.where(usable, double[:, None], jnp.zeros((), jnp.float32))
    return (usable, weight)


def crps_terms(ensemble, target_rows):
    members_count = ensemble.shape[0]
    offset = ensemble - target_rows[None]
    distance = soft_abs(offset)
    spread = jnp.sum(soft_abs(ensemble[:, None] - ensemble[None, :]), axis=1)
    pair_slope = jnp.sum(
        (ensemble[:, None] - ensemble[None, :]) / soft_abs(ensemble[:, None] - ensemble[None, :]),
        axis=1,
    )
    ens_score = jnp.mean(distance, axis=0) - 0.5 * jnp.mean(spread, axis=0) / members_count
    return (ens_score, offset / distance - pair_slope / members_count)


def body(members, target, target_spectrum, legendre, wavenum):
    ens_count = lax.axis_size("ens")
    lat_count = lax.axis_size("lat")
    ens_pos = lax.axis_index("ens")
    lat_pos = lax.axis_index("lat")
    batches = members.shape[1]
    var_local = members.shape[2]
    lat_rows = members.shape[3]
    longitudes = members.shape[4]
    slot_count = wavenum.shape[0]
    lat_slots = slot_count // lat_count
    dev_slots = lat_slots // ens_count
    latitudes = legendre.shape[1]
    degrees = legendre.shape[2]
    rows_each = lat_rows // ens_count
    member_rows = members.reshape(batches, 1, var_local, lat_rows, longitudes)
    regrouped = lax.all_to_all(member_rows, "ens", split_axis=3, concat_axis=1, tiled=True)
    target_rows = lax.dynamic_slice_in_dim(target, ens_pos * rows_each, rows_each, 2)

    def grid_item(paired):
        ens_score, point_slope = crps_terms(
            paired[0].astype(jnp.float32), paired[1].astype(jnp.float32)
        )
        return (jnp.mean(ens_score, axis=-1), point_slope.astype(jnp.bfloat16))

    row_score, grid_slope = lax.map(grid_item, (regrouped, target_rows))
    grid_back = lax.all_to_all(grid_slope, "ens", split_axis=1, concat_axis=3, tiled=True)
    lat_wave = lax.dynamic_slice_in_dim(wavenum, lat_pos * lat_slots, lat_slots)
    dev_wave = lax.dynamic_slice_in_dim(lat_wave, ens_pos * dev_slots, dev_slots)
    usable, weight = spectral_masks(dev_wave, degrees)
    flat_rows = members.reshape(batches * var_local * lat_rows, longitudes)
    natural_table = fourier_table(wavenum, longitudes)

    def spectral_item(paired):
        ens_score, point_slope = crps_terms(
            paired[0].astype(jnp.float32), paired[1].astype(jnp.float32)
        )
        scaled = weight[:, None, :]
        total = jnp.sum(ens_score * scaled, axis=(2, 3)) / (2.0 * (LMAX + 1))
        return (total, (point_slope * scaled).astype(jnp.bfloat16))

    reordered = (
        wavenum.reshape(lat_count, ens_count, dev_slots).transpose(1, 0, 2).reshape(slot_count)
    )
    along_lon = jnp.dot(
        flat_rows, fourier_table(reordered, longitudes), preferred_element_type=jnp.float32
    ).astype(jnp.bfloat16)
    along_lon = along_lon.reshape(batches, 1, var_local, lat_rows, 2 * slot_count)
    spread_fields = lax.all_to_all(
        lax.all_to_all(along_lon, "ens", split_axis=4, concat_axis=1, tiled=True),
        "lat",
        split_axis=4,
        concat_axis=3,
        tiled=True,
    )
    spread_fields = spread_fields.reshape(batches, ens_count, var_local, latitudes, dev_slots, 2)
    spectra = jnp.einsum(
        "stl,bmvtsc->bmvscl", legendre, spread_fields, preferred_element_type=jnp.float32
    )
    spectra = jnp.where(usable[:, None, :], spectra, 0.0).astype(jnp.bfloat16)
    spec_score, spec_slope = lax.map(spectral_item, (spectra, target_spectrum))
    along_back = jnp.einsum(
        "stl,bmvscl->bmvtsc", legendre, spec_slope, preferred_element_type=jnp.float32
    ).astype(jnp.bfloat16)
    along_back = along_back.reshape(batches, ens_count, var_local, latitudes, 2 * dev_slots)
    returned = lax.all_to_all(
        lax.all_to_all(along_back, "ens", split_axis=1, concat_axis=4, tiled=True),
        "lat",
        split_axis=3,
        concat_axis=4,
        tiled=True,
    )
    returned = returned.reshape(batches * var_local * lat_rows, 2 * slot_count)
    spectral_part = jnp.dot(returned, natural_table.T, preferred_element_type=jnp.float32)
    spectral_part = spectral_part.reshape(batches, var_local, lat_rows, longitudes)
    combined = (
        grid_back.reshape(batches, var_local, lat_rows, longitudes).astype(jnp.float32)
        + spectral_part
    )
    member_grad = combined.astype(jnp.bfloat16).reshape(1, batches, var_local, lat_rows, longitudes)
    return (member_grad, row_score, spec_score)


def solution(mesh):
    in_specs = (
        P("ens", None, "var", "lat", None),
        P(None, "var", "lat", None),
        P(None, "var", ("lat", "ens"), None, None),
        P(("lat", "ens"), None, None),
        P(),
    )
    out_specs = (
        P("ens", None, "var", "lat", None),
        P(None, "var", ("lat", "ens")),
        P(None, "var", ("lat", "ens")),
    )
    return jax.shard_map(body, mesh=mesh, in_specs=in_specs, out_specs=out_specs, check_vma=False)
```

profile of v0, /device:TPU:32, one launch (start us, length us, event | category | flops | bytes accessed | tf_op | source)
XLA Modules:
  0.0 573.4 jit_solution(16507684132270207352)
XLA Ops:
  0.6 1.7 reshape.342
  2.3 1.5 copy.94
  4.8 9.6 %multiply_convert_fusion.4 = (bf16[1440,384,1]{1,0,2:T(8,128)(2,1)S(1)}, bf16[1440,384,1]{1,0,2:T(8,128)(2,1)S(1)}) fusion(s32[384]{0:T(512)S(1)} %mul.230), kind=kLoop, calls=%fused_computation.68 | loop fusion | flops 7741440 | bytes 2213376 | tf_op jit(solution)/shard_map/convert.9
  14.4 1.6 pad_maximum_fusion
  16.1 6.8 %copy.95 = bf16[1440,384,2]{0,2,1:T(2,128)(2,1)} copy(bf16[1440,384,2]{1,0,2:T(8,128)(2,1)} %pad_maximum_fusion) | data formatting | bytes 4423680 | tf_op jit(solution)/shard_map/stack | solution.py:23
  22.9 6.0 %convert_element_type.182 = bf16[1440,768]{0,1:T(8,128)(2,1)} reshape(bf16[1440,384,2]{0,2,1:T(2,128)(2,1)} %copy.95) | data formatting | bytes 4423680 | tf_op jit(solution)/shard_map/convert_element_type | solution.py:24
  28.9 7.2 %fusion.24 = bf16[1152,768]{0,1:T(8,128)(2,1)} fusion(bf16[1440,768]{0,1:T(8,128)(2,1)} %convert_element_type.182, bf16[1152,1440]{1,0:T(8,128)(2,1)} %bitcast.137), kind=kOutput, calls=%fused_computation.53 | convolution fusion | flops 2548924416 | bytes 7299072 | tf_op jit(solution)/shard_map/dot_general | solution.py:92
  36.1 3.8 copy.96
  39.9 6.0 %copy.97 = bf16[3,1,6,64,768]{3,2,0,1,4:T(8,128)(2,1)} copy(bf16[3,1,6,64,768]{4,3,2,0,1:T(8,128)(2,1)} %bitcast.135) | data formatting | bytes 3538944 | tf_op jit(solution)/shard_map/reshape | solution.py:95
  45.9 7.6 %reshape.358 = bf16[16,2,27648]{2,1,0:T(2,128)(2,1)} reshape(bf16[768,1,3,6,64]{4,3,2,1,0:T(8,128)(2,1)} %bitcast.129) | data formatting | bytes 3538944
  53.5 52.7 %all_to_all.93 = bf16[16,2,27648]{2,1,0:T(2,128)(2,1)} all-to-all(bf16[16,2,27648]{2,1,0:T(2,128)(2,1)} %reshape.358), channel_id=1, replica_groups=mesh['ens'=16,'lat'=8,'var'=2] {'ens'}, dimensions={0} | all-to-all | bytes 3538944 | tf_op jit(solution)/shard_map/all_to_all | solution.py:97
  106.2 7.2 %reshape.359 = bf16[768,1,3,6,64]{4,3,2,1,0:T(8,128)(2,1)} reshape(bf16[16,2,27648]{2,1,0:T(2,128)(2,1)} %all_to_all.93) | data formatting | bytes 3538944
  113.5 8.2 %copy.142 = bf16[3,16,6,64,48]{3,1,2,0,4:T(8,128)(2,1)} copy(bf16[3,16,6,64,48]{3,2,0,4,1:T(8,128)(2,1)} %bitcast.131) | data formatting | bytes 3538944 | tf_op jit(solution)/shard_map/all_to_all | solution.py:97
  121.7 7.2 %reshape.360 = bf16[8,2,55296]{2,1,0:T(2,128)(2,1)} reshape(bf16[48,3,6,16,64]{4,3,2,1,0:T(8,128)(2,1)} %bitcast.133) | data formatting | bytes 3538944
  128.9 4.5 all-to-all-start.3
  133.4 6.1 %copy.140 = bf16[1,3,6,64,1440]{4,2,1,3,0:T(8,128)(2,1)} copy(bf16[1,3,6,64,1440]{4,3,2,1,0:T(8,128)(2,1)} %param.9) | data formatting | bytes 6635520 | tf_op args[0]
  140.9 16.2 %all-to-all-done.3 = bf16[8,2,55296]{2,1,0:T(2,128)(2,1)} async-done(((bf16[8,2,55296]{2,1,0:T(2,128)(2,1)}), bf16[8,2,55296]{2,1,0:T(2,128)(2,1)}, u32[]{:S(2)}, u32[]{:S(2)}) %all-to-all-start.3) | async-done | bytes 1769504 | tf_op jit(solution)/shard_map/all_to_all | solution.py:96
  157.2 5.0 all-to-all-start
  162.1 7.0 %reshape.361 = bf16[48,3,6,16,64]{4,3,2,1,0:T(8,128)(2,1)} reshape(bf16[8,2,55296]{2,1,0:T(2,128)(2,1)} %all-to-all-done.3) | data formatting | bytes 3538944
  169.1 7.9 %copy.101 = bf16[3,16,6,8,64,6]{4,3,1,5,2,0:T(8,128)(2,1)} copy(bf16[3,16,6,8,64,6]{4,1,2,0,5,3:T(8,128)(2,1)} %bitcast.132) | data formatting | bytes 3538944 | tf_op jit(solution)/shard_map/all_to_all | solution.py:96
  177.0 5.8 %reshape.345 = bf16[3,16,6,512,3,2]{3,1,5,4,2,0:T(8,128)(2,1)} reshape(bf16[3,16,6,8,64,6]{4,3,1,5,2,0:T(8,128)(2,1)} %copy.101) | data formatting | bytes 3538944 | tf_op jit(solution)/shard_map/reshape | solution.py:103
  182.8 4.0 fusion.40
  186.8 55.7 %while.34 = (s32[]{:T(128)}, f32[3,6,3]{1,2,0:T(4,128)}, bf16[3,16,6,3,2,384]{5,1,4,2,0,3:T(8,128)(2,1)}, bf16[3,16,6,3,2,384]{5,1,4,2,0,3:T(8,128)(2,1)}, bf16[...) while((s32[]{:T(128)}, f32[3,6,3]{1,2,0:T(4,128)}, ...), condition=%wide.region_11.12_spmd.clone, body=%wide.region_6.0_spmd.clone.sunk | while | flops 24388992 | bytes 10164653 | solution.py:108
  188.5 11.0 %fusion.54 = (f32[16,6,3,2,384]{4,3,2,1,0:T(2,128)S(1)}, f32[6,3,2,384]{3,2,1,0:T(2,128)S(1)}) fusion(f32[16,6,3,2,384]{4,0,3,2,1:T(8,128)S(1)} %copy.157, f32[16,6,3,2,384]{4,3,2,1,0:T(2,128)S(1)} %convert_bitcast_fusion.7), kind=kLoop, calls=%fused_computation.26.clone.1 | loop fusion | flops 20998656 | bytes 2709504 | tf_op jit(solution)/shard_map/while/body/eval_jaxpr/reduce_sum | solution.py:40
  203.0 1.6 sqrt_reduce_fusion.5
  207.0 11.0 %fusion.54 = (f32[16,6,3,2,384]{4,3,2,1,0:T(2,128)S(1)}, f32[6,3,2,384]{3,2,1,0:T(2,128)S(1)}) fusion(f32[16,6,3,2,384]{4,0,3,2,1:T(8,128)S(1)} %copy.157, f32[16,6,3,2,384]{4,3,2,1,0:T(2,128)S(1)} %convert_bitcast_fusion.7), kind=kLoop, calls=%fused_computation.26.clone.1 | loop fusion | flops 20998656 | bytes 2709504 | tf_op jit(solution)/shard_map/while/body/eval_jaxpr/reduce_sum | solution.py:40
  221.5 1.6 sqrt_reduce_fusion.5
  225.5 11.0 %fusion.54 = (f32[16,6,3,2,384]{4,3,2,1,0:T(2,128)S(1)}, f32[6,3,2,384]{3,2,1,0:T(2,128)S(1)}) fusion(f32[16,6,3,2,384]{4,0,3,2,1:T(8,128)S(1)} %copy.157, f32[16,6,3,2,384]{4,3,2,1,0:T(2,128)S(1)} %convert_bitcast_fusion.7), kind=kLoop, calls=%fused_computation.26.clone.1 | loop fusion | flops 20998656 | bytes 2709504 | tf_op jit(solution)/shard_map/while/body/eval_jaxpr/reduce_sum | solution.py:40
  240.0 1.6 sqrt_reduce_fusion.5
  242.5 2.8 convert_bitcast_fusion.3
  245.5 2.4 copy.106
  248.0 20.4 %all-to-all-done = bf16[3,1,6,64,1440]{4,2,0,1,3:T(8,128)(2,1)} async-done(((bf16[3,1,6,64,1440]{4,2,0,1,3:T(8,128)(2,1)}), bf16[3,1,6,64,1440]{4,2,0,1,3:T(8,128)(2,1)}, u32[]{:S(2)}, u32[]{:S(2)}) %all-to-all-start) | async-done | bytes 3317792 | tf_op jit(solution)/shard_map/all_to_all | solution.py:64
  268.4 8.2 %all-to-all-start.4 = ((bf16[3,16,6,512,6]{3,4,2,0,1:T(8,128)(2,1)}), bf16[3,16,6,512,6]{3,4,2,0,1:T(8,128)(2,1)}, u32[]{:S(2)}, u32[]{:S(2)}) async-start(bf16[3,16,6,512,6]{3,4,2,0,1:T(8,128)(2,1)} %copy.106), calls=%async_computation.4 | async-start | bytes 4718592 | tf_op jit(solution)/shard_map/all_to_all | solution.py:114
  277.4 4.2 copy.141
  281.6 49.6 %all-to-all-done.4 = bf16[3,16,6,512,6]{3,4,2,0,1:T(8,128)(2,1)} async-done(((bf16[3,16,6,512,6]{3,4,2,0,1:T(8,128)(2,1)}), bf16[3,16,6,512,6]{3,4,2,0,1:T(8,128)(2,1)}, u32[]{:S(2)}, u32[]{:S(2)}) %all-to-all-start.4) | async-done | bytes 1769504 | tf_op jit(solution)/shard_map/all_to_all | solution.py:114
  331.2 3.3 copy.107
  334.6 4.0 all_to_all.83
  338.5 4.6 copy.108
  343.1 4.6 all-to-all-start.5
  347.8 111.2 %while.33 = (s32[]{:T(128)}, f32[3,6,4]{1,2,0:T(4,128)S(1)}, bf16[3,16,6,4,1440]{4,3,2,0,1:T(4,128)(2,1)}, bf16[3,16,6,4,1440]{4,3,2,1,0:T(4,128)(2,1)S(1)}, bf16[3,6,4,1440]{3,2,1,0:T(4,128)(2,1)}, /*index=5*/s32[]{:T(128)}) while((s32[]{:T(128)}, f32[3,6,4]{1,2,0:T(4,128)S(1)}, bf16[3,16,6,4,1440]{4,3,2,0,1:T(4,128)(2,1)}, ...), condition=%wide.region_5.6_spmd, body=%wide.region_0.5_spmd.sunk | while | flops 60376320 | bytes 21022260 | solution.py:73
  348.4 1.4 copy.151
  349.8 29.2 %fusion.53 = (f32[16,6,4,1440]{3,2,1,0:T(4,128)S(1)}, f32[6,4,1440]{2,1,0:T(4,128)S(1)}) fusion(f32[16,6,4,1440]{3,0,2,1:T(8,128)S(1)} %copy.151, f32[16,6,4,1440]{3,2,1,0:T(4,128)S(1)} %convert_bitcast_fusion.6), kind=kLoop, calls=%fused_computation.6.clone.1 | loop fusion | flops 52496640 | bytes 6773760 | tf_op jit(solution)/shard_map/while/body/eval_jaxpr/reduce_sum | solution.py:40
  379.9 2.4 bitcast_dynamic-update-slice_fusion.7
  382.3 2.2 sqrt_reduce_fusion.4
  385.5 1.4 copy.151
  386.9 29.2 %fusion.53 = (f32[16,6,4,1440]{3,2,1,0:T(4,128)S(1)}, f32[6,4,1440]{2,1,0:T(4,128)S(1)}) fusion(f32[16,6,4,1440]{3,0,2,1:T(8,128)S(1)} %copy.151, f32[16,6,4,1440]{3,2,1,0:T(4,128)S(1)} %convert_bitcast_fusion.6), kind=kLoop, calls=%fused_computation.6.clone.1 | loop fusion | flops 52496640 | bytes 6773760 | tf_op jit(solution)/shard_map/while/body/eval_jaxpr/reduce_sum | solution.py:40
  417.0 2.4 bitcast_dynamic-update-slice_fusion.7
  419.4 2.2 sqrt_reduce_fusion.4
  423.9 29.2 %fusion.53 = (f32[16,6,4,1440]{3,2,1,0:T(4,128)S(1)}, f32[6,4,1440]{2,1,0:T(4,128)S(1)}) fusion(f32[16,6,4,1440]{3,0,2,1:T(8,128)S(1)} %copy.151, f32[16,6,4,1440]{3,2,1,0:T(4,128)S(1)} %convert_bitcast_fusion.6), kind=kLoop, calls=%fused_computation.6.clone.1 | loop fusion | flops 52496640 | bytes 6773760 | tf_op jit(solution)/shard_map/while/body/eval_jaxpr/reduce_sum | solution.py:40
  454.0 2.4 bitcast_dynamic-update-slice_fusion.7
  456.4 2.2 sqrt_reduce_fusion.4
  459.5 6.9 %all-to-all-start.1 = ((bf16[3,16,6,4,1440]{4,3,2,0,1:T(4,128)(2,1)}), bf16[3,16,6,4,1440]{4,3,2,0,1:T(4,128)(2,1)S(1)}, u32[]{:S(2)}, u32[]{:S(2)}) async-start(bf16[3,16,6,4,1440]{4,3,2,0,1:T(4,128)(2,1)} %get-tuple-element.230), calls=%async_computation.1 | async-start | bytes 7077888 | tf_op jit(solution)/shard_map/all_to_all | solution.py:74
  466.4 9.6 %multiply_convert_fusion.2 = (bf16[1440,384,1]{1,0,2:T(8,128)(2,1)S(1)}, bf16[1440,384,1]{1,0,2:T(8,128)(2,1)S(1)}) fusion(s32[384]{0:T(512)S(1)} %copy-done.2), kind=kLoop, calls=%fused_computation.63 | loop fusion | flops 7741440 | bytes 2213376 | tf_op jit(solution)/shard_map/convert.7
  476.1 1.6 pad_maximum_fusion.1
  477.7 6.9 %copy.111 = bf16[1440,384,2]{0,2,1:T(2,128)(2,1)} copy(bf16[1440,384,2]{1,0,2:T(8,128)(2,1)} %pad_maximum_fusion.1) | data formatting | bytes 4423680 | tf_op jit(solution)/shard_map/stack | solution.py:23
  484.6 6.0 %convert_element_type.190 = bf16[1440,768]{0,1:T(8,128)(2,1)} reshape(bf16[1440,384,2]{0,2,1:T(2,128)(2,1)} %copy.111) | data formatting | bytes 4423680 | tf_op jit(solution)/shard_map/convert_element_type | solution.py:24
  490.6 2.4 copy.109
  492.9 3.5 copy.110
  496.4 4.7 dot_general.17
  501.1 46.9 %all-to-all-done.1 = bf16[3,16,6,4,1440]{4,3,2,0,1:T(4,128)(2,1)S(1)} async-done(((bf16[3,16,6,4,1440]{4,3,2,0,1:T(4,128)(2,1)}), bf16[3,16,6,4,1440]{4,3,2,0,1:T(4,128)(2,1)S(1)}, u32[]{:S(2)}, u32[]{:S(2)}) %all-to-all-start.1) | async-done | bytes 3317792 | tf_op jit(solution)/shard_map/all_to_all | solution.py:74
  548.0 2.0 convert_bitcast_fusion.2
  550.1 4.8 copy.93
  554.8 9.0 %reshape.352 = f32[3,6,64,1440]{3,2,1,0:T(8,128)} reshape(f32[3,1,6,16,4,1440]{5,4,3,2,0,1:T(4,128)} %copy.93) | data formatting | bytes 13271040 | tf_op jit(solution)/shard_map/convert_element_type | solution.py:124
  563.9 9.1 %fusion.23 = bf16[1,3,6,64,1440]{4,3,2,1,0:T(8,128)(2,1)} fusion(f32[3,6,64,1440]{3,2,1,0:T(8,128)} %reshape.352, bf16[3,6,64,768]{3,2,1,0:T(8,128)(2,1)} %dot_general.17, bf16[1440,768]{0,1:T(8,128)(2,1)} %convert_element_type.190), kind=kOutput, calls=%fused_computation.49 | convolution fusion | flops 2551357440 | bytes 13934592 | tf_op jit(solution)/shard_map/dot_general | solution.py:121
  (71 shorter events, 28.3 us)
Async XLA Ops:
  0.6 276.0 %copy-start = (bf16[3,6,64,1440]{3,2,1,0:T(8,128)(2,1)S(1)}, bf16[3,6,64,1440]{3,2,1,0:T(8,128)(2,1)}, u32[]{:S(2)}) copy-start(bf16[3,6,64,1440]{3,2,1,0:T(8,128)(2,1)} %param.10) | copy-start | bytes 9953284
  128.9 28.3 %all-to-all-start.3 = ((bf16[8,2,55296]{2,1,0:T(2,128)(2,1)}), bf16[8,2,55296]{2,1,0:T(2,128)(2,1)}, u32[]{:S(2)}, u32[]{:S(2)}) async-start(bf16[8,2,55296]{2,1,0:T(2,128)(2,1)} %reshape.360), calls=%async_computation.3 | async-start | bytes 3538944 | tf_op jit(solution)/shard_map/all_to_all | solution.py:96
  157.2 111.3 %all-to-all-start = ((bf16[3,1,6,64,1440]{4,2,0,1,3:T(8,128)(2,1)}), bf16[3,1,6,64,1440]{4,2,0,1,3:T(8,128)(2,1)}, u32[]{:S(2)}, u32[]{:S(2)}) async-start(bf16[3,1,6,64,1440]{4,2,0,1,3:T(8,128)(2,1)} %bitcast.130), calls=%async_computation | async-start | bytes 9437184 | tf_op jit(solution)/shard_map/all_to_all | solution.py:64
  268.4 62.8 %all-to-all-start.4 = ((bf16[3,16,6,512,6]{3,4,2,0,1:T(8,128)(2,1)}), bf16[3,16,6,512,6]{3,4,2,0,1:T(8,128)(2,1)}, u32[]{:S(2)}, u32[]{:S(2)}) async-start(bf16[3,16,6,512,6]{3,4,2,0,1:T(8,128)(2,1)} %copy.106), calls=%async_computation.4 | async-start | bytes 4718592 | tf_op jit(solution)/shard_map/all_to_all | solution.py:114
  343.1 115.8 %all-to-all-start.5 = ((bf16[3,1,6,512,96]{4,2,0,1,3:T(8,128)(2,1)}), bf16[3,1,6,512,96]{4,2,0,1,3:T(8,128)(2,1)}, u32[]{:S(2)}, u32[]{:S(2)}) async-start(bf16[3,1,6,512,96]{4,2,0,1,3:T(8,128)(2,1)} %copy.108), calls=%async_computation.5 | async-start | bytes 6291456 | tf_op jit(solution)/shard_map/all_to_all | solution.py:113
  458.9 0.6 copy-start.3
  458.9 7.5 %copy-start.2 = (s32[384]{0:T(512)S(1)}, s32[384]{0:T(512)}, u32[]{:S(2)}) copy-start(s32[384]{0:T(512)} %param.13) | copy-start | bytes 4612
  459.5 88.5 %all-to-all-start.1 = ((bf16[3,16,6,4,1440]{4,3,2,0,1:T(4,128)(2,1)}), bf16[3,16,6,4,1440]{4,3,2,0,1:T(4,128)(2,1)S(1)}, u32[]{:S(2)}, u32[]{:S(2)}) async-start(bf16[3,16,6,4,1440]{4,3,2,0,1:T(4,128)(2,1)} %get-tuple-element.230), calls=%async_computation.1 | async-start | bytes 7077888 | tf_op jit(solution)/shard_map/all_to_all | solution.py:74
  563.9 9.1 %copy-start.1 = (bf16[3,6,64,1440]{3,2,1,0:T(8,128)(2,1)S(1)}, bf16[3,6,64,1440]{3,2,1,0:T(8,128)(2,1)}, u32[]{:S(2)}) copy-start(bf16[3,6,64,1440]{3,2,1,0:T(8,128)(2,1)} %param.10) | copy-start | bytes 9953284
where the time goes:
time: 583 us; the launch traced here: 573 us
  other arithmetic  180 us (31%)
  local copies, waits for them, and re-layouts  154 us (26%)
  waiting for transfers between devices  133 us (23%)
  blocking collectives  52.7 us (9%)
  starting transfers between devices  29.1 us (5%)
  matrix products  23 us (4%)
    reduce_sum x6, other arithmetic, crps_terms(): jnp.sum((ensemble[:, None] - ensemble[None, :]) / soft_abs(ensemble[:, No...  121 us
    all_to_all x1, blocking collectives, body(): lax.all_to_all(along_lon, 'ens', split_axis=4, concat_axis=1, tiled=True)  52.7 us
    all_to_all x1, waiting for transfers between devices, body(): lax.all_to_all(along_back, 'ens', split_axis=1, concat_axis=4, tiled=True)  49.6 us
    all_to_all x1, waiting for transfers between devices, body(): lax.all_to_all(grid_slope, 'ens', split_axis=1, concat_axis=3, tiled=True)  46.9 us
    unnamed x13, local copies, waits for them, and re-layouts  35.8 us
    all_to_all x1, waiting for transfers between devices, body(): lax.all_to_all(member_rows, 'ens', split_axis=3, concat_axis=1, tiled=True)  20.4 us
    another operation x2, other arithmetic  19.2 us
    all_to_all x1, waiting for transfers between devices, body(): lax.all_to_all(lax.all_to_all(along_lon, 'ens', split_axis=4, concat_axis...  16.2 us
  transfers between devices with their start and end apart: 5, of which 4 were waited for; matrix products, arithmetic and copies ran while one was open for 43% of the time, Pallas kernels for 0%

commit v1 on v0

v1 whole, which is shorter than its diff:
```python
import functools
import math

import jax
import jax.numpy as jnp
from jax import lax
from jax.experimental import pallas as pl
from jax.experimental.pallas import tpu as pltpu
from jax.sharding import PartitionSpec as P

LMAX = 360
MESH = pl.DeviceIdType.MESH
F32 = jnp.float32
BF16 = jnp.bfloat16
WIDTH2 = 0.0625

ENS = 16
LATS = 8
FIELDS = 18
BAND = 64
ROWS = FIELDS * BAND
LON = 1440
SLOTS = 384
COLS = 2 * SLOTS
DEV_SLOTS = 3
PARTS = 2 * DEV_SLOTS
LATITUDES = 512
DEGREES = 384
PAIRS = FIELDS // 2
FULL = LON // 128
TAIL = LON - FULL * 128
BLOCKS = BAND // 16
FIELD_TILES = BLOCKS * FULL + 1
TILES = FIELDS * FIELD_TILES
OWN = -(-TILES // ENS)
CHUNKS = ((0, 17), (17, 17), (34, 17))
ENTRIES = FIELDS * PARTS
GROUPS = -(-ENTRIES // 8)


def crps_block(x, y):
    offset = x - y[None]
    square = offset * offset + WIDTH2
    inverse = lax.rsqrt(square)
    near = jnp.sum(square * inverse, axis=0)
    slope = jnp.zeros_like(x)
    spread = jnp.zeros_like(y)
    half = ENS // 2
    for shift in range(1, half):
        d = x - jnp.concatenate([x[shift:], x[:shift]], axis=0)
        s = d * d + WIDTH2
        r = lax.rsqrt(s)
        spread = spread + jnp.sum(s * r, axis=0)
        ratio = d * r
        back = jnp.concatenate([ratio[ENS - shift:], ratio[: ENS - shift]], axis=0)
        slope = slope + (ratio - back)
    d = x[:half] - x[half:]
    s = d * d + WIDTH2
    r = lax.rsqrt(s)
    spread = spread + jnp.sum(s * r, axis=0)
    ratio = d * r
    slope = slope + jnp.concatenate([ratio, -ratio], axis=0)
    pair_mean = (2.0 * spread + ENS * math.sqrt(WIDTH2)) * (0.5 / (ENS * ENS))
    return near * (1.0 / ENS) - pair_mean, offset * inverse - slope * (1.0 / ENS)


def body_kernel(
    mem, tgt, tsp, leg, waves, wnum,
    out, row_out, spec_out,
    tiles, own_target, got_a, got_d, table, send, got_b1, got_b2, got_c1, got_c2,
    wide, mixed, spectral, tspec, spec_sum, part, xs, ys, scores, score_sum, got_s,
    a_send, a_recv, d_send, d_recv, b1_send, b1_recv, b2_send, b2_recv,
    c1_send, c1_recv, c2_send, c2_recv, s_send, s_recv, own_sem,
):
    e = lax.axis_index("ens")
    q_me = lax.axis_index("lat")

    def ens_peer(k):
        return lax.rem(e + k, ENS)

    def lat_peer(k):
        return lax.rem(q_me + k, LATS)

    barrier = pltpu.get_barrier_semaphore()

    def greet_ens(k, carry):
        pl.semaphore_signal(barrier, inc=1, device_id={"ens": ens_peer(k)}, device_id_type=MESH)
        return carry

    def greet_lat(k, carry):
        pl.semaphore_signal(barrier, inc=1, device_id={"lat": lat_peer(k)}, device_id_type=MESH)
        return carry

    lax.fori_loop(1, ENS, greet_ens, 0)
    lax.fori_loop(1, LATS, greet_lat, 0)

    def retile(field, carry):
        rows = pl.multiple_of(field * BAND, BAND)
        for block in range(BLOCKS):
            for lane in range(FULL):
                tiles[field * FIELD_TILES + block * FULL + lane] = mem[
                    pl.ds(rows + 16 * block, 16), pl.ds(lane * 128, 128)
                ]
        tails = [
            mem[pl.ds(rows + 16 * block, 16), pl.ds(FULL * 128, TAIL)].astype(F32)
            for block in range(BLOCKS)
        ]
        tiles[field * FIELD_TILES + FIELD_TILES - 1] = jnp.concatenate(tails, axis=1).astype(BF16)
        return carry

    lax.fori_loop(0, FIELDS, retile, 0)
    tiles[pl.ds(TILES, ENS * OWN - TILES)] = jnp.zeros((ENS * OWN - TILES, 16, 128), BF16)

    def a_copy(chunk, peer, slot):
        first, count = CHUNKS[chunk]
        return pltpu.make_async_remote_copy(
            src_ref=tiles.at[pl.ds(peer * OWN + first, count)],
            dst_ref=got_a.at[slot, pl.ds(first, count)],
            send_sem=a_send.at[chunk, peer],
            recv_sem=a_recv.at[chunk, slot],
            device_id={"ens": peer},
            device_id_type=MESH,
        )

    def a_start(chunk):
        def step(k, carry):
            a_copy(chunk, ens_peer(k), e).start()
            return carry

        lax.fori_loop(1, ENS, step, 0)

    def a_wait(chunk):
        def step(k, carry):
            a_copy(chunk, e, ens_peer(k)).wait_recv()
            return carry

        lax.fori_loop(1, ENS, step, 0)

    pl.semaphore_wait(barrier, ENS - 1 + LATS - 1)
    a_start(0)
    own_copy = pltpu.make_async_copy(tiles.at[pl.ds(e * OWN, OWN)], got_a.at[e], own_sem)
    own_copy.start()

    def table_rows(index, carry):
        rows = pl.ds(pl.multiple_of(index * 64, 64), 64)
        wave = waves[rows, :].astype(F32)
        lane = lax.broadcasted_iota(jnp.int32, (64, 128), 1).astype(F32)
        row = lax.broadcasted_iota(jnp.int32, (64, 128), 0)

        def angles(turns):
            turns = turns - LON * jnp.floor(turns * (1.0 / LON))
            return turns * (2.0 * math.pi / LON)

        fine = angles(wave * lane)
        coarse = angles(wave * (128.0 * jnp.minimum(lane, 15.0)))
        cos_b, sin_b = jnp.cos(fine), jnp.sin(fine)
        factor = 1.0 / math.sqrt(LON)
        cos_a, sin_a = jnp.cos(coarse) * factor, jnp.sin(coarse) * factor
        real = lax.rem(row, 2) == 0
        first = jnp.where(real, cos_a, -sin_a)
        second = jnp.where(real, -sin_a, -cos_a)
        for lane_block in range(FULL + 1):
            width = min(128, LON - lane_block * 128)
            value = first[:, lane_block : lane_block + 1] * cos_b
            value = value + second[:, lane_block : lane_block + 1] * sin_b
            table[rows, pl.ds(lane_block * 128, width)] = value[:, :width].astype(BF16)
        return carry

    lax.fori_loop(0, COLS // 64, table_rows, 0)

    def forward(index, carry):
        lanes = pl.ds(pl.multiple_of(index * 384, 384), 384)
        value = lax.dot_general(
            table[...], mem[lanes, :], (((1,), (1,)), ((), ())), preferred_element_type=F32
        )
        send[:, lanes] = value.astype(BF16)
        return carry

    lax.fori_loop(0, ROWS // 384, forward, 0)

    per_lat = COLS // LATS
    per_ens = COLS // ENS

    def lat_copy(source, got, s_sem, r_sem, peer, slot):
        return pltpu.make_async_remote_copy(
            src_ref=source.at[pl.ds(peer * per_lat, per_lat)],
            dst_ref=got.at[pl.ds(slot * per_lat, per_lat)],
            send_sem=s_sem.at[peer],
            recv_sem=r_sem.at[slot],
            device_id={"lat": peer},
            device_id_type=MESH,
        )

    def ens_copy(source, got, s_sem, r_sem, peer, slot):
        return pltpu.make_async_remote_copy(
            src_ref=source.at[pl.ds(peer * per_ens, per_ens)],
            dst_ref=got.at[pl.ds(slot * per_ens, per_ens)],
            send_sem=s_sem.at[peer],
            recv_sem=r_sem.at[slot],
            device_id={"ens": peer},
            device_id_type=MESH,
        )

    def exchange(copy, count, peer_of, me, size, got, s_sem, r_sem):
        def start(k, carry):
            copy(send, got, s_sem, r_sem, peer_of(k), me).start()
            return carry

        lax.fori_loop(1, count, start, 0)
        mine = pl.ds(pl.multiple_of(me * size, size), size)
        got[mine, :] = send[mine, :]

    def finish(copy, count, peer_of, me, got, s_sem, r_sem):
        def wait(k, carry):
            copy(send, got, s_sem, r_sem, peer_of(k), me).wait_send()
            copy(send, got, s_sem, r_sem, me, peer_of(k)).wait_recv()
            return carry

        lax.fori_loop(1, count, wait, 0)

    def widen(got):
        def step(index, carry):
            rows = pl.ds(pl.multiple_of(index * 48, 48), 48)
            for pair in range(PAIRS):
                wide[pair, rows, :] = got[rows, pl.ds(pair * 128, 128)].astype(F32)
            return carry

        lax.fori_loop(0, COLS // 48, step, 0)

    exchange(lat_copy, LATS, lat_peer, q_me, per_lat, got_b1, b1_send, b1_recv)

    def target_tile(index, carry):
        tile = e * OWN + index
        field = tile // FIELD_TILES
        place = tile - field * FIELD_TILES

        @pl.when(jnp.logical_and(place < FIELD_TILES - 1, tile < TILES))
        def _():
            block = place // FULL
            lane = place - block * FULL
            rows = pl.multiple_of(field * BAND + block * 16, 16)
            own_target[index] = tgt[
                pl.ds(rows, 16), pl.ds(pl.multiple_of(lane * 128, 128), 128)
            ].astype(F32)

        @pl.when(jnp.logical_and(place == FIELD_TILES - 1, tile < TILES))
        def _():
            rows = pl.multiple_of(field * BAND, BAND)
            tails = [
                tgt[pl.ds(rows + 16 * block, 16), pl.ds(FULL * 128, TAIL)].astype(F32)
                for block in range(BLOCKS)
            ]
            own_target[index] = jnp.concatenate(tails, axis=1)

        @pl.when(tile >= TILES)
        def _():
            own_target[index] = jnp.zeros((16, 128), F32)

        return carry

    lax.fori_loop(0, OWN, target_tile, 0)
    field_first = (e * OWN) // FIELD_TILES
    scores[...] = jnp.zeros_like(scores)
    tspec[pl.ds(0, ENTRIES), :] = tsp[...].astype(F32)
    tspec[pl.ds(ENTRIES, GROUPS * 8 - ENTRIES), :] = jnp.zeros((GROUPS * 8 - ENTRIES, DEGREES), F32)
    spec_sum[...] = jnp.zeros_like(spec_sum)

    finish(lat_copy, LATS, lat_peer, q_me, got_b1, b1_send, b1_recv)
    widen(got_b1)

    def regroup_b(peer, carry):
        for pair in range(PAIRS):
            for twin in range(PARTS // 2):
                start = peer * PARTS + 2 * twin
                value = jnp.concatenate(
                    [
                        wide[pair, pl.ds(start, LATS, stride=per_lat), :],
                        wide[pair, pl.ds(start + 1, LATS, stride=per_lat), :],
                    ],
                    axis=0,
                )
                rows = pl.multiple_of(peer * per_ens + 16 * twin, 16)
                send[pl.ds(rows, 16), pl.ds(pair * 128, 128)] = value.astype(BF16)
        return carry

    lax.fori_loop(0, ENS, regroup_b, 0)
    exchange(ens_copy, ENS, ens_peer, e, per_ens, got_b2, b2_send, b2_recv)

    def grid_tile(index, carry):
        def load(member, inner):
            xs[member] = got_a[member, index].astype(F32)
            return inner

        lax.fori_loop(0, ENS, load, 0, unroll=True)
        for top in (0, 8):
            rows = pl.ds(top, 8)
            score, slope = crps_block(xs[:, rows, :], own_target[index, rows, :])
            ys[:, rows, :] = slope
            part[rows, :] = score

        def store(member, inner):
            got_a[member, index] = ys[member].astype(BF16)
            return inner

        lax.fori_loop(0, ENS, store, 0, unroll=True)
        tile = e * OWN + index
        field = tile // FIELD_TILES
        place = tile - field * FIELD_TILES
        local = field - field_first

        @pl.when(place < FIELD_TILES - 1)
        def _():
            rows = pl.ds(pl.multiple_of(place // FULL * 16, 16), 16)
            scores[local, rows, :] = scores[local, rows, :] + part[...]

        @pl.when(place == FIELD_TILES - 1)
        def _():
            segment = lax.broadcasted_iota(jnp.int32, (16, 128), 1) // TAIL
            for block in range(BLOCKS):
                rows = pl.ds(16 * block, 16)
                scores[local, rows, :] = scores[local, rows, :] + jnp.where(
                    segment == block, part[...], 0.0
                )

        return carry

    def d_copy(chunk, peer, slot):
        first, count = CHUNKS[chunk]
        return pltpu.make_async_remote_copy(
            src_ref=got_a.at[peer, pl.ds(first, count)],
            dst_ref=got_d.at[pl.ds(slot * OWN + first, count)],
            send_sem=d_send.at[chunk, peer],
            recv_sem=d_recv.at[chunk, slot],
            device_id={"ens": peer},
            device_id_type=MESH,
        )

    def d_start(chunk):
        def step(k, carry):
            d_copy(chunk, ens_peer(k), e).start()
            return carry

        lax.fori_loop(1, ENS, step, 0)

    def grid_chunk(chunk):
        a_wait(chunk)
        first, count = CHUNKS[chunk]
        lax.fori_loop(first, first + count, grid_tile, 0)

    own_copy.wait()
    grid_chunk(0)

    finish(ens_copy, ENS, ens_peer, e, got_b2, b2_send, b2_recv)
    a_start(1)
    a_start(2)
    widen(got_b2)
    low = lax.broadcasted_iota(jnp.int32, (16, 128), 1) < 64

    def swap(even, odd):
        first = jnp.where(low, even, pltpu.roll(odd, 64, 1))
        second = jnp.where(low, pltpu.roll(even, 64, 1), odd)
        return first, second

    half_rows = 2 * PAIRS * ENS

    def legendre_in(index, carry):
        pair = index // PARTS
        piece = index - pair * PARTS
        slot = piece // 2
        c = piece - 2 * slot
        row = pl.multiple_of((c * PAIRS + pair) * ENS, ENS)
        for twin in range(LATS // 2):
            start = piece * LATS + 2 * twin
            even = wide[pair, pl.ds(start, ENS, stride=per_ens), :]
            odd = wide[pair, pl.ds(start + 1, ENS, stride=per_ens), :]
            first, second = swap(even, odd)
            mixed[slot, pl.ds(row, ENS), pl.ds(twin * 128, 128)] = first.astype(BF16)
            mixed[slot, pl.ds(row + half_rows, ENS), pl.ds(twin * 128, 128)] = second.astype(BF16)
        return carry

    lax.fori_loop(0, PAIRS * PARTS, legendre_in, 0)
    for lane_block in range(DEGREES // 128):
        spectral[lane_block, pl.ds(ENTRIES * ENS, GROUPS * 8 * ENS - ENTRIES * ENS), :] = jnp.zeros(
            (GROUPS * 8 * ENS - ENTRIES * ENS, 128), F32
        )

    def analysis(slot, carry):
        value = jnp.dot(mixed[slot], leg[slot], preferred_element_type=F32)
        for field in range(FIELDS):
            for c in range(2):
                row = (field % 2) * half_rows + (c * PAIRS + field // 2) * ENS
                to = pl.multiple_of((field * PARTS + 2 * slot + c) * ENS, ENS)
                for lane_block in range(DEGREES // 128):
                    spectral[lane_block, pl.ds(to, ENS), :] = value[
                        row : row + ENS, lane_block * 128 : lane_block * 128 + 128
                    ]
        return carry

    lax.fori_loop(0, DEV_SLOTS, analysis, 0)

    first_slot = (q_me * ENS + e) * DEV_SLOTS
    slot_waves = [wnum[first_slot + s] for s in range(DEV_SLOTS)]

    def spectral_group(index, carry):
        group = index // (DEGREES // 128)
        lane_block = index - group * (DEGREES // 128)
        entry = group * 8 + lax.broadcasted_iota(jnp.int32, (8, 128), 0)
        slot = lax.rem(entry // 2, DEV_SLOTS)
        wave = jnp.where(slot == 0, slot_waves[0], jnp.where(slot == 1, slot_waves[1], slot_waves[2]))
        degree = lane_block * 128 + lax.broadcasted_iota(jnp.int32, (8, 128), 1)
        usable = jnp.logical_and(degree >= wave, degree <= LMAX)
        weight = jnp.where(usable, jnp.where(wave == 0, 1.0, 2.0), 0.0)
        base = group * (8 * ENS)
        x = jnp.stack(
            [spectral[lane_block, pl.ds(base + m, 8, stride=ENS), :] for m in range(ENS)], axis=0
        )
        x = jnp.where(usable[None], x, 0.0).astype(BF16).astype(F32)
        rows = pl.ds(pl.multiple_of(group * 8, 8), 8)
        y = tspec[rows, pl.ds(pl.multiple_of(lane_block * 128, 128), 128)]
        score, slope = crps_block(x, y)
        spec_sum[rows, :] = spec_sum[rows, :] + score * weight
        slope = slope * weight[None]
        for m in range(ENS):
            spectral[lane_block, pl.ds(base + m, 8, stride=ENS), :] = slope[m]
        return carry

    lax.fori_loop(0, GROUPS * (DEGREES // 128), spectral_group, 0)

    def synthesis(slot, carry):
        for field in range(FIELDS):
            for c in range(2):
                row = (field % 2) * half_rows + (c * PAIRS + field // 2) * ENS
                at = pl.multiple_of((field * PARTS + 2 * slot + c) * ENS, ENS)
                for lane_block in range(DEGREES // 128):
                    mixed[slot, pl.ds(row, ENS), pl.ds(lane_block * 128, 128)] = spectral[
                        lane_block, pl.ds(at, ENS), :
                    ].astype(BF16)
        value = lax.dot_general(
            mixed[slot, :, pl.ds(0, DEGREES)], leg[slot], (((1,), (1,)), ((), ())),
            preferred_element_type=F32,
        )
        for pair in range(PAIRS):
            for c in range(2):
                row = (c * PAIRS + pair) * ENS
                for twin in range(LATS // 2):
                    lanes = slice(twin * 128, twin * 128 + 128)
                    even, odd = swap(
                        value[row : row + ENS, lanes],
                        value[row + half_rows : row + half_rows + ENS, lanes],
                    )
                    start = (2 * slot + c) * LATS + 2 * twin
                    wide[pair, pl.ds(start, ENS, stride=per_ens), :] = even
                    wide[pair, pl.ds(start + 1, ENS, stride=per_ens), :] = odd
        return carry

    lax.fori_loop(0, DEV_SLOTS, synthesis, 0)

    def narrow(index, carry):
        rows = pl.ds(pl.multiple_of(index * 48, 48), 48)
        for pair in range(PAIRS):
            send[rows, pl.ds(pair * 128, 128)] = wide[pair, rows, :].astype(BF16)
        return carry

    lax.fori_loop(0, COLS // 48, narrow, 0)
    exchange(ens_copy, ENS, ens_peer, e, per_ens, got_c1, c1_send, c1_recv)
    d_start(0)

    for chunk in range(1, len(CHUNKS)):
        grid_chunk(chunk)
        d_start(chunk)
    own_back = pltpu.make_async_copy(got_a.at[e], got_d.at[pl.ds(e * OWN, OWN)], own_sem)
    own_back.start()

    lane = lax.broadcasted_iota(jnp.int32, (BAND, 128), 1)
    total = jnp.zeros((BAND, 128), F32)
    for local in range(3):
        rows_sum = jnp.sum(scores[local], axis=1, keepdims=True) * (1.0 / LON)
        total = total + jnp.where(lane == field_first + local, rows_sum, 0.0)
    score_sum[...] = total.reshape(LATS, 8, 128)

    def s_copy(peer, slot):
        return pltpu.make_async_remote_copy(
            src_ref=score_sum.at[peer // 2],
            dst_ref=got_s.at[slot],
            send_sem=s_send.at[peer],
            recv_sem=s_recv.at[slot],
            device_id={"ens": peer},
            device_id_type=MESH,
        )

    def s_start(k, carry):
        s_copy(ens_peer(k), e).start()
        return carry

    lax.fori_loop(1, ENS, s_start, 0)
    got_s[e] = score_sum[e // 2]

    finish(ens_copy, ENS, ens_peer, e, got_c1, c1_send, c1_recv)
    widen(got_c1)

    def regroup_c(band, carry):
        rows = pl.ds(pl.multiple_of(band * per_lat, per_lat), per_lat)
        for pair in range(PAIRS):
            send[rows, pl.ds(pair * 128, 128)] = wide[
                pair, pl.ds(band, per_lat, stride=LATS), :
            ].astype(BF16)
        return carry

    lax.fori_loop(0, LATS, regroup_c, 0)
    exchange(lat_copy, LATS, lat_peer, q_me, per_lat, got_c2, c2_send, c2_recv)
    spec_out[...] = jnp.sum(spec_sum[...], axis=1, keepdims=True) * (1.0 / (2.0 * (LMAX + 1)))
    finish(lat_copy, LATS, lat_peer, q_me, got_c2, c2_send, c2_recv)

    def d_wait(chunk):
        def step(k, carry):
            d_copy(chunk, ens_peer(k), e).wait_send()
            d_copy(chunk, e, ens_peer(k)).wait_recv()
            a_copy(chunk, ens_peer(k), e).wait_send()
            return carry

        lax.fori_loop(1, ENS, step, 0)

    def s_wait(k, carry):
        s_copy(ens_peer(k), e).wait_send()
        s_copy(e, ens_peer(k)).wait_recv()
        return carry

    for chunk in range(len(CHUNKS)):
        d_wait(chunk)
    lax.fori_loop(1, ENS, s_wait, 0)
    own_back.wait()
    row_out[...] = jnp.sum(got_s[...], axis=0)

    def backward(index, carry):
        lanes = pl.ds(pl.multiple_of(index * 128, 128), 128)
        value = lax.dot_general(
            got_c2[:, lanes], table[...], (((0,), (0,)), ((), ())), preferred_element_type=F32
        )
        for twin in range(2):
            field = 2 * index + twin
            rows = pl.multiple_of(field * BAND, BAND)
            tail = got_d[field * FIELD_TILES + FIELD_TILES - 1].astype(F32)
            for block in range(BLOCKS):
                at = twin * BAND + block * 16
                for lane_block in range(FULL):
                    both = value[at : at + 16, lane_block * 128 : lane_block * 128 + 128]
                    both = both + got_d[field * FIELD_TILES + block * FULL + lane_block].astype(F32)
                    out[pl.ds(rows + 16 * block, 16), pl.ds(lane_block * 128, 128)] = both.astype(BF16)
                moved = tail if block == 0 else pltpu.roll(tail, 128 - block * TAIL, 1)
                both = value[at : at + 16, FULL * 128 :] + moved[:, :TAIL]
                out[pl.ds(rows + 16 * block, 16), pl.ds(FULL * 128, TAIL)] = both.astype(BF16)
        return carry

    lax.fori_loop(0, PAIRS, backward, 0)


def body(members, target, target_spectrum, legendre, wavenum):
    ens_pos = lax.axis_index("ens")
    chunks = len(CHUNKS)
    vmem = pl.BlockSpec(memory_space=pltpu.VMEM)
    dma = pltpu.SemaphoreType.DMA
    member_grad, rows, spec = pl.pallas_call(
        body_kernel,
        out_shape=(
            jax.ShapeDtypeStruct((ROWS, LON), BF16),
            jax.ShapeDtypeStruct((8, 128), F32),
            jax.ShapeDtypeStruct((GROUPS * 8, 1), F32),
        ),
        in_specs=[vmem] * 5 + [pl.BlockSpec(memory_space=pltpu.SMEM)],
        out_specs=(vmem, vmem, vmem),
        scratch_shapes=[
            pltpu.VMEM((ENS * OWN, 16, 128), BF16),
            pltpu.VMEM((OWN, 16, 128), F32),
            pltpu.VMEM((ENS, OWN, 16, 128), BF16),
            pltpu.VMEM((ENS * OWN, 16, 128), BF16),
            pltpu.VMEM((COLS, LON), BF16),
            pltpu.VMEM((COLS, ROWS), BF16),
            pltpu.VMEM((COLS, ROWS), BF16),
            pltpu.VMEM((COLS, ROWS), BF16),
            pltpu.VMEM((COLS, ROWS), BF16),
            pltpu.VMEM((COLS, ROWS), BF16),
            pltpu.VMEM((PAIRS, COLS, 128), F32),
            pltpu.VMEM((DEV_SLOTS, FIELDS * 2 * ENS, LATITUDES), BF16),
            pltpu.VMEM((DEGREES // 128, GROUPS * 8 * ENS, 128), F32),
            pltpu.VMEM((GROUPS * 8, DEGREES), F32),
            pltpu.VMEM((GROUPS * 8, 128), F32),
            pltpu.VMEM((16, 128), F32),
            pltpu.VMEM((ENS, 16, 128), F32),
            pltpu.VMEM((ENS, 16, 128), F32),
            pltpu.VMEM((3, BAND, 128), F32),
            pltpu.VMEM((LATS, 8, 128), F32),
            pltpu.VMEM((ENS, 8, 128), F32),
            dma((chunks, ENS)), dma((chunks, ENS)),
            dma((chunks, ENS)), dma((chunks, ENS)),
            dma((LATS,)), dma((LATS,)),
            dma((ENS,)), dma((ENS,)),
            dma((ENS,)), dma((ENS,)),
            dma((LATS,)), dma((LATS,)),
            dma((ENS,)), dma((ENS,)),
            dma,
        ],
        compiler_params=pltpu.CompilerParams(
            collective_id=0, has_side_effects=True, vmem_limit_bytes=60 * 2**20
        ),
    )(
        members.reshape(ROWS, LON),
        target.reshape(ROWS, LON),
        target_spectrum.reshape(ENTRIES, DEGREES),
        legendre,
        jnp.repeat(wavenum, 2).reshape(COLS, 1),
        wavenum,
    )
    batches, fields = members.shape[1], members.shape[2]
    member_grad = member_grad.reshape(members.shape)
    own = lax.dynamic_slice_in_dim(rows, lax.rem(ens_pos, 2) * 4, 4, 0)[:, :FIELDS]
    row_score = own.T.reshape(batches, fields, 4)
    spec = spec.reshape(-1)[:ENTRIES].reshape(FIELDS, DEV_SLOTS, 2)
    spec_score = (spec[..., 0] + spec[..., 1]).reshape(batches, fields, DEV_SLOTS)
    return (member_grad, row_score, spec_score)


def solution(mesh):
    in_specs = (
        P("ens", None, "var", "lat", None),
        P(None, "var", "lat", None),
        P(None, "var", ("lat", "ens"), None, None),
        P(("lat", "ens"), None, None),
        P(),
    )
    out_specs = (
        P("ens", None, "var", "lat", None),
        P(None, "var", ("lat", "ens")),
        P(None, "var", ("lat", "ens")),
    )
    return jax.shard_map(body, mesh=mesh, in_specs=in_specs, out_specs=out_specs, check_vma=False)
```

time: 583 us -> 275 us (0.47)
  Pallas kernels: 0 us -> 258 us
  other arithmetic: 180 us -> 0.09 us
  local copies, waits for them, and re-layouts: 154 us -> 10.7 us
  waiting for transfers between devices: 133 us -> 0 us
  blocking collectives: 52.7 us -> 0 us
  starting transfers between devices: 29.1 us -> 0 us
  matrix products: 23 us -> 0 us
    pallas_call x0 -> x1, Pallas kernels: none -> 258 us  [body(): pl.pallas_call(body_kernel, out_shape=(jax.ShapeDtypeStruct((ROWS, LON),...]
    all_to_all x5 -> x0, waiting for transfers between devices: 133 us -> none  [the longest x1 49.6 us: body(): lax.all_to_all(along_back, 'ens', split_axis=1, concat_axis=4, tiled=True)]
    reduce_sum x18 -> x0, other arithmetic: 133 us -> none  [the longest x6 121 us: crps_terms(): jnp.sum((ensemble[:, None] - ensemble[None, :]) / soft_abs(ensemble[:, No...]
    all_to_all x1 -> x0, blocking collectives: 52.7 us -> none  [body(): lax.all_to_all(along_lon, 'ens', split_axis=4, concat_axis=1, tiled=True)]
    all_to_all x8 -> x0, local copies, waits for them, and re-layouts: 38 us -> none  [the longest x3 11.9 us: body(): lax.all_to_all(along_back, 'ens', split_axis=1, concat_axis=4, tiled=True)]
    convert_element_type x12 -> x0, local copies, waits for them, and re-layouts: 34.3 us -> none  [the longest x2 13.8 us: body(): grid_back.reshape(batches, var_local, lat_rows, longitudes)]
    unnamed x13 -> x3, local copies, waits for them, and re-layouts: 35.8 us -> 5.3 us
    all_to_all x5 -> x0, starting transfers between devices: 29.1 us -> none  [the longest x1 8.18 us: body(): lax.all_to_all(along_back, 'ens', split_axis=1, concat_axis=4, tiled=True)]
  transfers between devices with their start and end apart: 5 -> 0, of which waited for: 4 -> 0; matrix products, arithmetic and copies ran while one was open for 43% -> 0% of each run, Pallas kernels for 0% -> 0%
where the time goes in v1:
time: 275 us; the launch traced here: 269 us
  Pallas kernels  258 us (94%)
  local copies, waits for them, and re-layouts  10.7 us (4%)
    pallas_call x1, Pallas kernels, body(): pl.pallas_call(body_kernel, out_shape=(jax.ShapeDtypeStruct((ROWS, LON),...  258 us

profile of v1, /device:TPU:32, one launch (start us, length us, event | category | flops | bytes accessed | tf_op | source)
XLA Modules:
  0.0 269.3 jit_solution(9549404018017841142)
XLA Ops:
  0.6 1.6 reshape.33.tsp
  2.3 0.8 broadcast_in_dim.3
  3.1 0.9 reshape_reshape.4.waves
  3.9 257.9 %shard_map.76 = (bf16[1152,1440]{1,0:T(8,128)(2,1)}, f32[8,128]{1,0:T(8,128)}, f32[112,1]{1,0:T(8,128)}) custom-call(bf16[1152,1440]{1,0:T(8,128)(2,1)} %bitcast.9, bf16[1152,1440]{1,0:T(8,128)(2,1)} %bitcast.10, bf16[108,384]{1,0:T(8,128)(2,1)} %reshape.33.tsp, bf16[3,512,384]{2,1,0:T(8,128)(2,1)} %leg.1, s32[768,1]{1,0:T(8,128)} %reshape_reshape.4.waves, ...), custom_call_target="tpu_custom_call" | custom-call | tf_op jit(solution)/shard_map/pallas_call | solution.py:562
  261.8 0.7 constant_dynamic-slice_fusion
  262.5 0.1 reshape.35
  262.6 0.6 copy.13
  263.2 0.9 slice_reduce_fusion
  264.1 0.2 reshape.36
  264.3 0.1 slice_add_fusion
  264.4 0.1 copy.12
  264.5 0.1 add.12
  264.6 0.6 copy.14
  265.2 4.1 %copy.16 = bf16[1,3,6,64,1440]{4,3,2,1,0:T(8,128)(2,1)} copy(bf16[1,3,6,64,1440]{4,3,2,1,0:T(8,128)(2,1)} %bitcast.11) | data formatting | bytes 6635520
  (1 shorter events, 0.0 us)

commit v2 on v1

--- a/solution.py
+++ b/solution.py
@@ -15,8 +15,12 @@
 WIDTH2 = 0.0625
 
 ENS = 16
+ZS = 8
+XS = 2
 LATS = 8
+PLANE = LATS * XS
 FIELDS = 18
+BATCHES = 3
 BAND = 64
 ROWS = FIELDS * BAND
 LON = 1440
@@ -33,7 +37,9 @@
 FIELD_TILES = BLOCKS * FULL + 1
 TILES = FIELDS * FIELD_TILES
 OWN = -(-TILES // ENS)
-CHUNKS = ((0, 17), (17, 17), (34, 17))
+CHUNKS = ((0, 9), (9, 18), (27, 24))
+LOADS = 3
+STEPS = 6
 ENTRIES = FIELDS * PARTS
 GROUPS = -(-ENTRIES // 8)
 
@@ -65,12 +71,12 @@
 
 
 def body_kernel(
-    mem, tgt, tsp, leg, waves, wnum,
-    out, row_out, spec_out,
-    tiles, own_target, got_a, got_d, table, send, got_b1, got_b2, got_c1, got_c2,
+    mem_hbm, tgt_hbm, tsp, leg_hbm, wave_rows, wnum,
+    got_d, grad_hbm, small,
+    mem, tgt, leg, tiles, own_target, got_a, stage_a, stage_d, grad, table, send, got_b1, got_b2, got_c1, got_c2,
     wide, mixed, spectral, tspec, spec_sum, part, xs, ys, scores, score_sum, got_s,
-    a_send, a_recv, d_send, d_recv, b1_send, b1_recv, b2_send, b2_recv,
-    c1_send, c1_recv, c2_send, c2_recv, s_send, s_recv, own_sem,
+    ax_send, ax_recv, dx_send, dx_recv, a_send, a_recv, d_send, d_recv, b1_send, b1_recv, b2_send, b2_recv,
+    c1_send, c1_recv, c2_send, c2_recv, s_send, s_recv, mem_sem, tgt_sem, leg_sem, grad_sem, keep_sem,
 ):
     e = lax.axis_index("ens")
     q_me = lax.axis_index("lat")
@@ -78,21 +84,45 @@
     def ens_peer(k):
         return lax.rem(e + k, ENS)
 
-    def lat_peer(k):
-        return lax.rem(q_me + k, LATS)
-
+    x_me = e // ZS
+    z_me = e - x_me * ZS
+    partner = (1 - x_me) * ZS + z_me
+    g_me = q_me * XS + x_me
+
+    def z_peer(k):
+        return lax.rem(z_me + k, ZS)
+
+    def plane_peer(k):
+        return lax.rem(g_me + k, PLANE)
+
+    def mem_load(index):
+        rows = pl.ds(index * (ROWS // LOADS), ROWS // LOADS)
+        return pltpu.make_async_copy(mem_hbm.at[rows], mem.at[rows], mem_sem.at[index])
+
+    tgt_load = pltpu.make_async_copy(tgt_hbm, tgt, tgt_sem)
+    leg_load = pltpu.make_async_copy(leg_hbm, leg, leg_sem)
+    for index in range(LOADS):
+        mem_load(index).start()
+    tgt_load.start()
+    leg_load.start()
     barrier = pltpu.get_barrier_semaphore()
 
     def greet_ens(k, carry):
         pl.semaphore_signal(barrier, inc=1, device_id={"ens": ens_peer(k)}, device_id_type=MESH)
         return carry
 
-    def greet_lat(k, carry):
-        pl.semaphore_signal(barrier, inc=1, device_id={"lat": lat_peer(k)}, device_id_type=MESH)
+    def greet_plane(k, carry):
+        for x in range(XS):
+            pl.semaphore_signal(
+                barrier,
+                inc=1,
+                device_id={"ens": x * ZS + z_me, "lat": lax.rem(q_me + k, LATS)},
+                device_id_type=MESH,
+            )
         return carry
 
     lax.fori_loop(1, ENS, greet_ens, 0)
-    lax.fori_loop(1, LATS, greet_lat, 0)
+    lax.fori_loop(1, LATS, greet_plane, 0)
 
     def retile(field, carry):
         rows = pl.multiple_of(field * BAND, BAND)
@@ -108,44 +138,109 @@
         tiles[field * FIELD_TILES + FIELD_TILES - 1] = jnp.concatenate(tails, axis=1).astype(BF16)
         return carry
 
-    lax.fori_loop(0, FIELDS, retile, 0)
+    for index in range(LOADS):
+        mem_load(index).wait()
+        lax.fori_loop(index * (FIELDS // LOADS), (index + 1) * (FIELDS // LOADS), retile, 0)
     tiles[pl.ds(TILES, ENS * OWN - TILES)] = jnp.zeros((ENS * OWN - TILES, 16, 128), BF16)
 
-    def a_copy(chunk, peer, slot):
+    def ax_copy(chunk, z):
         first, count = CHUNKS[chunk]
         return pltpu.make_async_remote_copy(
-            src_ref=tiles.at[pl.ds(peer * OWN + first, count)],
+            src_ref=tiles.at[pl.ds(((1 - x_me) * ZS + z) * OWN + first, count)],
+            dst_ref=stage_a.at[z, pl.ds(first, count)],
+            send_sem=ax_send.at[chunk, z],
+            recv_sem=ax_recv.at[chunk, z],
+            device_id={"ens": partner},
+            device_id_type=MESH,
+        )
+
+    def a_copy(chunk, z, slot):
+        first, count = CHUNKS[chunk]
+        return pltpu.make_async_remote_copy(
+            src_ref=tiles.at[pl.ds((x_me * ZS + z) * OWN + first, count)],
             dst_ref=got_a.at[slot, pl.ds(first, count)],
-            send_sem=a_send.at[chunk, peer],
+            send_sem=a_send.at[chunk, z],
             recv_sem=a_recv.at[chunk, slot],
-            device_id={"ens": peer},
+            device_id={"ens": x_me * ZS + z},
             device_id_type=MESH,
         )
+
+    def a_pass(chunk, z, slot):
+        first, count = CHUNKS[chunk]
+        return pltpu.make_async_remote_copy(
+            src_ref=stage_a.at[z, pl.ds(first, count)],
+            dst_ref=got_a.at[slot, pl.ds(first, count)],
+            send_sem=a_send.at[chunk, ZS + z],
+            recv_sem=a_recv.at[chunk, slot],
+            device_id={"ens": x_me * ZS + z},
+            device_id_type=MESH,
+        )
+
+    def ax_start(chunk):
+        def step(k, carry):
+            ax_copy(chunk, z_peer(k)).start()
+            return carry
+
+        lax.fori_loop(1, ZS + 1, step, 0)
 
     def a_start(chunk):
         def step(k, carry):
-            a_copy(chunk, ens_peer(k), e).start()
-            return carry
-
-        lax.fori_loop(1, ENS, step, 0)
+            a_copy(chunk, z_peer(k), e).start()
+            return carry
+
+        lax.fori_loop(1, ZS, step, 0)
+        first, count = CHUNKS[chunk]
+        got_a[e, pl.ds(first, count)] = tiles[pl.ds(e * OWN + first, count)]
+
+    def a_forward(chunk):
+        def step(k, carry):
+            ax_copy(chunk, z_peer(k)).wait_recv()
+            a_pass(chunk, z_peer(k), partner).start()
+            return carry
+
+        lax.fori_loop(1, ZS, step, 0)
+        ax_copy(chunk, z_me).wait_recv()
+        first, count = CHUNKS[chunk]
+        got_a[partner, pl.ds(first, count)] = stage_a[z_me, pl.ds(first, count)]
 
     def a_wait(chunk):
         def step(k, carry):
-            a_copy(chunk, e, ens_peer(k)).wait_recv()
-            return carry
-
-        lax.fori_loop(1, ENS, step, 0)
-
-    pl.semaphore_wait(barrier, ENS - 1 + LATS - 1)
-    a_start(0)
-    own_copy = pltpu.make_async_copy(tiles.at[pl.ds(e * OWN, OWN)], got_a.at[e], own_sem)
-    own_copy.start()
+            a_copy(chunk, z_me, x_me * ZS + z_peer(k)).wait_recv()
+            a_pass(chunk, z_me, (1 - x_me) * ZS + z_peer(k)).wait_recv()
+            return carry
+
+        lax.fori_loop(1, ZS, step, 0)
+
+    def a_done(chunk):
+        def step(k, carry):
+            a_copy(chunk, z_peer(k), e).wait_send()
+            a_pass(chunk, z_peer(k), partner).wait_send()
+            return carry
+
+        def step_x(z, carry):
+            ax_copy(chunk, z).wait_send()
+            return carry
+
+        lax.fori_loop(1, ZS, step, 0)
+        lax.fori_loop(0, ZS, step_x, 0)
+
+    pl.semaphore_wait(barrier, ENS - 1 + XS * (LATS - 1))
+    for chunk in range(len(CHUNKS)):
+        a_start(chunk)
+        if chunk == 0:
+            ax_start(0)
 
     def table_rows(index, carry):
         rows = pl.ds(pl.multiple_of(index * 64, 64), 64)
-        wave = waves[rows, :].astype(F32)
         lane = lax.broadcasted_iota(jnp.int32, (64, 128), 1).astype(F32)
         row = lax.broadcasted_iota(jnp.int32, (64, 128), 0)
+        group = wave_rows[pl.ds(index // 4, 1), :].astype(F32)
+        at = lax.rem(index, 4) * 32 + row // 2
+        wave = jnp.sum(
+            jnp.where(lax.broadcasted_iota(jnp.int32, (64, 128), 1) == at, group, 0.0),
+            axis=1,
+            keepdims=True,
+        )
 
         def angles(turns):
             turns = turns - LON * jnp.floor(turns * (1.0 / LON))
@@ -178,26 +273,26 @@
 
     lax.fori_loop(0, ROWS // 384, forward, 0)
 
-    per_lat = COLS // LATS
-    per_ens = COLS // ENS
-
-    def lat_copy(source, got, s_sem, r_sem, peer, slot):
+    per_plane = COLS // PLANE
+    per_z = COLS // ZS
+
+    def plane_copy(source, got, s_sem, r_sem, peer, slot):
         return pltpu.make_async_remote_copy(
-            src_ref=source.at[pl.ds(peer * per_lat, per_lat)],
-            dst_ref=got.at[pl.ds(slot * per_lat, per_lat)],
+            src_ref=source.at[pl.ds(peer * per_plane, per_plane)],
+            dst_ref=got.at[pl.ds(slot * per_plane, per_plane)],
             send_sem=s_sem.at[peer],
             recv_sem=r_sem.at[slot],
-            device_id={"lat": peer},
+            device_id={"ens": lax.rem(peer, XS) * ZS + z_me, "lat": peer // XS},
             device_id_type=MESH,
         )
 
-    def ens_copy(source, got, s_sem, r_sem, peer, slot):
+    def z_copy(source, got, s_sem, r_sem, peer, slot):
         return pltpu.make_async_remote_copy(
-            src_ref=source.at[pl.ds(peer * per_ens, per_ens)],
-            dst_ref=got.at[pl.ds(slot * per_ens, per_ens)],
+            src_ref=source.at[pl.ds(peer * per_z, per_z)],
+            dst_ref=got.at[pl.ds(slot * per_z, per_z)],
             send_sem=s_sem.at[peer],
             recv_sem=r_sem.at[slot],
-            device_id={"ens": peer},
+            device_id={"ens": x_me * ZS + peer},
             device_id_type=MESH,
         )
 
@@ -227,7 +322,9 @@
 
         lax.fori_loop(0, COLS // 48, step, 0)
 
-    exchange(lat_copy, LATS, lat_peer, q_me, per_lat, got_b1, b1_send, b1_recv)
+    exchange(plane_copy, PLANE, plane_peer, g_me, per_plane, got_b1, b1_send, b1_recv)
+
+    tgt_load.wait()
 
     def target_tile(index, carry):
         tile = e * OWN + index
@@ -261,30 +358,30 @@
     lax.fori_loop(0, OWN, target_tile, 0)
     field_first = (e * OWN) // FIELD_TILES
     scores[...] = jnp.zeros_like(scores)
-    tspec[pl.ds(0, ENTRIES), :] = tsp[...].astype(F32)
+    for b in range(BATCHES):
+        for v in range(FIELDS // BATCHES):
+            for s in range(DEV_SLOTS):
+                row = (b * (FIELDS // BATCHES) + v) * PARTS + 2 * s
+                tspec[pl.ds(row, 2), :] = tsp[b, v, s].astype(F32)
     tspec[pl.ds(ENTRIES, GROUPS * 8 - ENTRIES), :] = jnp.zeros((GROUPS * 8 - ENTRIES, DEGREES), F32)
     spec_sum[...] = jnp.zeros_like(spec_sum)
 
-    finish(lat_copy, LATS, lat_peer, q_me, got_b1, b1_send, b1_recv)
+    a_forward(0)
+    finish(plane_copy, PLANE, plane_peer, g_me, got_b1, b1_send, b1_recv)
     widen(got_b1)
 
     def regroup_b(peer, carry):
         for pair in range(PAIRS):
-            for twin in range(PARTS // 2):
-                start = peer * PARTS + 2 * twin
-                value = jnp.concatenate(
-                    [
-                        wide[pair, pl.ds(start, LATS, stride=per_lat), :],
-                        wide[pair, pl.ds(start + 1, LATS, stride=per_lat), :],
-                    ],
-                    axis=0,
-                )
-                rows = pl.multiple_of(peer * per_ens + 16 * twin, 16)
-                send[pl.ds(rows, 16), pl.ds(pair * 128, 128)] = value.astype(BF16)
-        return carry
-
-    lax.fori_loop(0, ENS, regroup_b, 0)
-    exchange(ens_copy, ENS, ens_peer, e, per_ens, got_b2, b2_send, b2_recv)
+            for piece in range(PARTS):
+                value = wide[pair, pl.ds(peer * PARTS + piece, PLANE, stride=per_plane), :]
+                rows = pl.multiple_of(peer * per_z + PLANE * piece, PLANE)
+                send[pl.ds(rows, PLANE), pl.ds(pair * 128, 128)] = value.astype(BF16)
+        return carry
+
+    lax.fori_loop(0, ZS, regroup_b, 0)
+    exchange(z_copy, ZS, z_peer, z_me, per_z, got_b2, b2_send, b2_recv)
+    ax_start(1)
+    ax_start(2)
 
     def grid_tile(index, carry):
         def load(member, inner):
@@ -324,35 +421,108 @@
 
         return carry
 
-    def d_copy(chunk, peer, slot):
+    def dx_copy(chunk, z):
         first, count = CHUNKS[chunk]
         return pltpu.make_async_remote_copy(
-            src_ref=got_a.at[peer, pl.ds(first, count)],
+            src_ref=got_a.at[(1 - x_me) * ZS + z, pl.ds(first, count)],
+            dst_ref=stage_d.at[z, pl.ds(first, count)],
+            send_sem=dx_send.at[chunk, z],
+            recv_sem=dx_recv.at[chunk, z],
+            device_id={"ens": partner},
+            device_id_type=MESH,
+        )
+
+    def d_copy(chunk, z, slot):
+        first, count = CHUNKS[chunk]
+        return pltpu.make_async_remote_copy(
+            src_ref=got_a.at[x_me * ZS + z, pl.ds(first, count)],
             dst_ref=got_d.at[pl.ds(slot * OWN + first, count)],
-            send_sem=d_send.at[chunk, peer],
+            send_sem=d_send.at[chunk, z],
             recv_sem=d_recv.at[chunk, slot],
-            device_id={"ens": peer},
+            device_id={"ens": x_me * ZS + z},
             device_id_type=MESH,
         )
+
+    def d_pass(chunk, z, slot):
+        first, count = CHUNKS[chunk]
+        return pltpu.make_async_remote_copy(
+            src_ref=stage_d.at[z, pl.ds(first, count)],
+            dst_ref=got_d.at[pl.ds(slot * OWN + first, count)],
+            send_sem=d_send.at[chunk, ZS + z],
+            recv_sem=d_recv.at[chunk, slot],
+            device_id={"ens": x_me * ZS + z},
+            device_id_type=MESH,
+        )
+
+    def d_keep(chunk):
+        first, count = CHUNKS[chunk]
+        return pltpu.make_async_copy(
+            got_a.at[e, pl.ds(first, count)],
+            got_d.at[pl.ds(e * OWN + first, count)],
+            keep_sem.at[chunk, 0],
+        )
+
+    def d_cross(chunk):
+        first, count = CHUNKS[chunk]
+        return pltpu.make_async_copy(
+            stage_d.at[z_me, pl.ds(first, count)],
+            got_d.at[pl.ds(partner * OWN + first, count)],
+            keep_sem.at[chunk, 1],
+        )
+
+    def dx_start(chunk):
+        def step(k, carry):
+            dx_copy(chunk, z_peer(k)).start()
+            return carry
+
+        lax.fori_loop(1, ZS + 1, step, 0)
 
     def d_start(chunk):
         def step(k, carry):
-            d_copy(chunk, ens_peer(k), e).start()
-            return carry
-
-        lax.fori_loop(1, ENS, step, 0)
+            d_copy(chunk, z_peer(k), e).start()
+            return carry
+
+        lax.fori_loop(1, ZS, step, 0)
+        d_keep(chunk).start()
+
+    def d_forward(chunk):
+        def step(k, carry):
+            dx_copy(chunk, z_peer(k)).wait_recv()
+            d_pass(chunk, z_peer(k), partner).start()
+            return carry
+
+        lax.fori_loop(1, ZS, step, 0)
+        dx_copy(chunk, z_me).wait_recv()
+        d_cross(chunk).start()
+
+    def d_wait(chunk):
+        def step(k, carry):
+            d_copy(chunk, z_peer(k), e).wait_send()
+            d_pass(chunk, z_peer(k), partner).wait_send()
+            d_copy(chunk, z_me, x_me * ZS + z_peer(k)).wait_recv()
+            d_pass(chunk, z_me, (1 - x_me) * ZS + z_peer(k)).wait_recv()
+            return carry
+
+        def step_x(z, carry):
+            dx_copy(chunk, z).wait_send()
+            return carry
+
+        lax.fori_loop(1, ZS, step, 0)
+        lax.fori_loop(0, ZS, step_x, 0)
+        d_keep(chunk).wait()
+        d_cross(chunk).wait()
 
     def grid_chunk(chunk):
         a_wait(chunk)
         first, count = CHUNKS[chunk]
         lax.fori_loop(first, first + count, grid_tile, 0)
 
-    own_copy.wait()
     grid_chunk(0)
-
-    finish(ens_copy, ENS, ens_peer, e, got_b2, b2_send, b2_recv)
-    a_start(1)
-    a_start(2)
+    dx_start(0)
+
+    a_forward(1)
+    finish(z_copy, ZS, z_peer, z_me, got_b2, b2_send, b2_recv)
+    a_forward(2)
     widen(got_b2)
     low = lax.broadcasted_iota(jnp.int32, (16, 128), 1) < 64
 
@@ -370,9 +540,10 @@
         c = piece - 2 * slot
         row = pl.multiple_of((c * PAIRS + pair) * ENS, ENS)
         for twin in range(LATS // 2):
-            start = piece * LATS + 2 * twin
-            even = wide[pair, pl.ds(start, ENS, stride=per_ens), :]
-            odd = wide[pair, pl.ds(start + 1, ENS, stride=per_ens), :]
+            start = piece * PLANE + 2 * XS * twin
+            rows = [wide[pair, pl.ds(start + i, ZS, stride=per_z), :] for i in range(2 * XS)]
+            even = jnp.concatenate(rows[:XS], axis=0)
+            odd = jnp.concatenate(rows[XS:], axis=0)
             first, second = swap(even, odd)
             mixed[slot, pl.ds(row, ENS), pl.ds(twin * 128, 128)] = first.astype(BF16)
             mixed[slot, pl.ds(row + half_rows, ENS), pl.ds(twin * 128, 128)] = second.astype(BF16)
@@ -383,6 +554,8 @@
         spectral[lane_block, pl.ds(ENTRIES * ENS, GROUPS * 8 * ENS - ENTRIES * ENS), :] = jnp.zeros(
             (GROUPS * 8 * ENS - ENTRIES * ENS, 128), F32
         )
+
+    leg_load.wait()
 
     def analysis(slot, carry):
         value = jnp.dot(mixed[slot], leg[slot], preferred_element_type=F32)
@@ -448,9 +621,11 @@
                         value[row : row + ENS, lanes],
                         value[row + half_rows : row + half_rows + ENS, lanes],
                     )
-                    start = (2 * slot + c) * LATS + 2 * twin
-                    wide[pair, pl.ds(start, ENS, stride=per_ens), :] = even
-                    wide[pair, pl.ds(start + 1, ENS, stride=per_ens), :] = odd
+                    start = (2 * slot + c) * PLANE + 2 * XS * twin
+                    for i in range(XS):
+                        members = slice(i * ZS, i * ZS + ZS)
+                        wide[pair, pl.ds(start + i, ZS, stride=per_z), :] = even[members]
+                        wide[pair, pl.ds(start + XS + i, ZS, stride=per_z), :] = odd[members]
         return carry
 
     lax.fori_loop(0, DEV_SLOTS, synthesis, 0)
@@ -462,14 +637,16 @@
         return carry
 
     lax.fori_loop(0, COLS // 48, narrow, 0)
-    exchange(ens_copy, ENS, ens_peer, e, per_ens, got_c1, c1_send, c1_recv)
+    exchange(z_copy, ZS, z_peer, z_me, per_z, got_c1, c1_send, c1_recv)
     d_start(0)
-
-    for chunk in range(1, len(CHUNKS)):
-        grid_chunk(chunk)
-        d_start(chunk)
-    own_back = pltpu.make_async_copy(got_a.at[e], got_d.at[pl.ds(e * OWN, OWN)], own_sem)
-    own_back.start()
+    grid_chunk(1)
+    dx_start(1)
+    d_start(1)
+    d_forward(0)
+    grid_chunk(2)
+    dx_start(2)
+    d_start(2)
+    d_forward(1)
 
     lane = lax.broadcasted_iota(jnp.int32, (BAND, 128), 1)
     total = jnp.zeros((BAND, 128), F32)
@@ -495,30 +672,45 @@
     lax.fori_loop(1, ENS, s_start, 0)
     got_s[e] = score_sum[e // 2]
 
-    finish(ens_copy, ENS, ens_peer, e, got_c1, c1_send, c1_recv)
+    d_forward(2)
+    finish(z_copy, ZS, z_peer, z_me, got_c1, c1_send, c1_recv)
     widen(got_c1)
 
-    def regroup_c(band, carry):
-        rows = pl.ds(pl.multiple_of(band * per_lat, per_lat), per_lat)
+    def regroup_c(place, carry):
+        rows = pl.ds(pl.multiple_of(place * per_plane, per_plane), per_plane)
         for pair in range(PAIRS):
             send[rows, pl.ds(pair * 128, 128)] = wide[
-                pair, pl.ds(band, per_lat, stride=LATS), :
+                pair, pl.ds(place, per_plane, stride=PLANE), :
             ].astype(BF16)
         return carry
 
-    lax.fori_loop(0, LATS, regroup_c, 0)
-    exchange(lat_copy, LATS, lat_peer, q_me, per_lat, got_c2, c2_send, c2_recv)
-    spec_out[...] = jnp.sum(spec_sum[...], axis=1, keepdims=True) * (1.0 / (2.0 * (LMAX + 1)))
-    finish(lat_copy, LATS, lat_peer, q_me, got_c2, c2_send, c2_recv)
-
-    def d_wait(chunk):
-        def step(k, carry):
-            d_copy(chunk, ens_peer(k), e).wait_send()
-            d_copy(chunk, e, ens_peer(k)).wait_recv()
-            a_copy(chunk, ens_peer(k), e).wait_send()
-            return carry
-
-        lax.fori_loop(1, ENS, step, 0)
+    lax.fori_loop(0, PLANE, regroup_c, 0)
+    exchange(plane_copy, PLANE, plane_peer, g_me, per_plane, got_c2, c2_send, c2_recv)
+    sums = jnp.sum(spec_sum[...], axis=1, keepdims=True) * (1.0 / (2.0 * (LMAX + 1)))
+    entry = lax.broadcasted_iota(jnp.int32, (GROUPS * 8, 128), 0)
+    variables = FIELDS // BATCHES
+    place = lax.broadcasted_iota(jnp.int32, (GROUPS * 8, 128), 1)
+    sums = jnp.where(place == lax.rem(entry // PARTS, variables), sums, 0.0)
+    for b in range(BATCHES):
+        for slot in range(DEV_SLOTS):
+            chosen = jnp.logical_and(
+                entry // (PARTS * variables) == b, lax.rem(entry, PARTS) // 2 == slot
+            )
+            small[pl.ds(8 + b * DEV_SLOTS + slot, 1), :] = jnp.sum(
+                jnp.where(chosen, sums, 0.0), axis=0, keepdims=True
+            )
+    finish(plane_copy, PLANE, plane_peer, g_me, got_c2, c2_send, c2_recv)
+
+    def backward(index, carry):
+        lanes = pl.ds(pl.multiple_of(index * 384, 384), 384)
+        grad[lanes, :] = lax.dot_general(
+            got_c2[:, lanes], table[...], (((0,), (0,)), ((), ())), preferred_element_type=F32
+        )
+        return carry
+
+    lax.fori_loop(0, ROWS // 384, backward, 0)
+    grad_store = pltpu.make_async_copy(grad, grad_hbm, grad_sem)
+    grad_store.start()
 
     def s_wait(k, carry):
         s_copy(ens_peer(k), e).wait_send()
@@ -526,53 +718,65 @@
         return carry
 
     for chunk in range(len(CHUNKS)):
+        a_done(chunk)
+    for chunk in range(len(CHUNKS)):
         d_wait(chunk)
     lax.fori_loop(1, ENS, s_wait, 0)
-    own_back.wait()
-    row_out[...] = jnp.sum(got_s[...], axis=0)
-
-    def backward(index, carry):
-        lanes = pl.ds(pl.multiple_of(index * 128, 128), 128)
-        value = lax.dot_general(
-            got_c2[:, lanes], table[...], (((0,), (0,)), ((), ())), preferred_element_type=F32
-        )
-        for twin in range(2):
-            field = 2 * index + twin
-            rows = pl.multiple_of(field * BAND, BAND)
-            tail = got_d[field * FIELD_TILES + FIELD_TILES - 1].astype(F32)
-            for block in range(BLOCKS):
-                at = twin * BAND + block * 16
-                for lane_block in range(FULL):
-                    both = value[at : at + 16, lane_block * 128 : lane_block * 128 + 128]
-                    both = both + got_d[field * FIELD_TILES + block * FULL + lane_block].astype(F32)
-                    out[pl.ds(rows + 16 * block, 16), pl.ds(lane_block * 128, 128)] = both.astype(BF16)
-                moved = tail if block == 0 else pltpu.roll(tail, 128 - block * TAIL, 1)
-                both = value[at : at + 16, FULL * 128 :] + moved[:, :TAIL]
-                out[pl.ds(rows + 16 * block, 16), pl.ds(FULL * 128, TAIL)] = both.astype(BF16)
-        return carry
-
-    lax.fori_loop(0, PAIRS, backward, 0)
+    rows = jnp.sum(got_s[...], axis=0)
+    small[pl.ds(0, 4), :] = jnp.where(lax.rem(e, 2) == 0, rows[:4], rows[4:])
+    grad_store.wait()
+
+
+def combine_kernel(got_d, grad, small, out, row_out, spec_out):
+    variables = FIELDS // BATCHES
+
+    @pl.when(pl.program_id(0) == 0)
+    def _():
+        for b in range(BATCHES):
+            row_out[b] = small[pl.ds(0, 4), pl.ds(b * variables, variables)]
+            spec_out[b] = small[pl.ds(8 + b * DEV_SLOTS, DEV_SLOTS), pl.ds(0, variables)]
+
+    def combine(field, carry):
+        top = pl.multiple_of(field * BAND, BAND)
+        tail = got_d[field * FIELD_TILES + FIELD_TILES - 1].astype(F32)
+        for block in range(BLOCKS):
+            rows = pl.ds(top + 16 * block, 16)
+            for lane_block in range(FULL):
+                lanes = pl.ds(lane_block * 128, 128)
+                slope = got_d[field * FIELD_TILES + block * FULL + lane_block].astype(F32)
+                out[rows, lanes] = (grad[rows, lanes] + slope).astype(BF16)
+            lanes = pl.ds(FULL * 128, TAIL)
+            moved = tail if block == 0 else pltpu.roll(tail, 128 - block * TAIL, 1)
+            out[rows, lanes] = (grad[rows, lanes] + moved[:, :TAIL]).astype(BF16)
+        return carry
+
+    lax.fori_loop(0, FIELDS // STEPS, combine, 0)
 
 
 def body(members, target, target_spectrum, legendre, wavenum):
-    ens_pos = lax.axis_index("ens")
     chunks = len(CHUNKS)
     vmem = pl.BlockSpec(memory_space=pltpu.VMEM)
+    hbm = pl.BlockSpec(memory_space=pl.ANY)
     dma = pltpu.SemaphoreType.DMA
-    member_grad, rows, spec = pl.pallas_call(
+    slopes, grad, small = pl.pallas_call(
         body_kernel,
         out_shape=(
-            jax.ShapeDtypeStruct((ROWS, LON), BF16),
-            jax.ShapeDtypeStruct((8, 128), F32),
-            jax.ShapeDtypeStruct((GROUPS * 8, 1), F32),
+            jax.ShapeDtypeStruct((ENS * OWN, 16, 128), BF16),
+            jax.ShapeDtypeStruct((ROWS, LON), F32),
+            jax.ShapeDtypeStruct((24, 128), F32),
         ),
-        in_specs=[vmem] * 5 + [pl.BlockSpec(memory_space=pltpu.SMEM)],
-        out_specs=(vmem, vmem, vmem),
+        in_specs=[hbm, hbm, vmem, hbm, vmem, pl.BlockSpec(memory_space=pltpu.SMEM)],
+        out_specs=(hbm, hbm, vmem),
         scratch_shapes=[
+            pltpu.VMEM((ROWS, LON), BF16),
+            pltpu.VMEM((ROWS, LON), BF16),
+            pltpu.VMEM((DEV_SLOTS, LATITUDES, DEGREES), BF16),
             pltpu.VMEM((ENS * OWN, 16, 128), BF16),
             pltpu.VMEM((OWN, 16, 128), F32),
             pltpu.VMEM((ENS, OWN, 16, 128), BF16),
-            pltpu.VMEM((ENS * OWN, 16, 128), BF16),
+            pltpu.VMEM((ZS, OWN, 16, 128), BF16),
+            pltpu.VMEM((ZS, OWN, 16, 128), BF16),
+            pltpu.VMEM((ROWS, LON), F32),
             pltpu.VMEM((COLS, LON), BF16),
             pltpu.VMEM((COLS, ROWS), BF16),
             pltpu.VMEM((COLS, ROWS), BF16),
@@ -590,14 +794,16 @@
             pltpu.VMEM((3, BAND, 128), F32),
             pltpu.VMEM((LATS, 8, 128), F32),
             pltpu.VMEM((ENS, 8, 128), F32),
+            dma((chunks, ZS)), dma((chunks, ZS)),
+            dma((chunks, ZS)), dma((chunks, ZS)),
             dma((chunks, ENS)), dma((chunks, ENS)),
             dma((chunks, ENS)), dma((chunks, ENS)),
-            dma((LATS,)), dma((LATS,)),
+            dma((PLANE,)), dma((PLANE,)),
+            dma((ZS,)), dma((ZS,)),
+            dma((ZS,)), dma((ZS,)),
+            dma((PLANE,)), dma((PLANE,)),
             dma((ENS,)), dma((ENS,)),
-            dma((ENS,)), dma((ENS,)),
-            dma((LATS,)), dma((LATS,)),
-            dma((ENS,)), dma((ENS,)),
-            dma,
+            dma((LOADS,)), dma, dma, dma, dma((chunks, 2)),
         ],
         compiler_params=pltpu.CompilerParams(
             collective_id=0, has_side_effects=True, vmem_limit_bytes=60 * 2**20
@@ -605,18 +811,38 @@
     )(
         members.reshape(ROWS, LON),
         target.reshape(ROWS, LON),
-        target_spectrum.reshape(ENTRIES, DEGREES),
+        target_spectrum,
         legendre,
-        jnp.repeat(wavenum, 2).reshape(COLS, 1),
+        wavenum.reshape(SLOTS // 128, 128),
         wavenum,
     )
-    batches, fields = members.shape[1], members.shape[2]
-    member_grad = member_grad.reshape(members.shape)
-    own = lax.dynamic_slice_in_dim(rows, lax.rem(ens_pos, 2) * 4, 4, 0)[:, :FIELDS]
-    row_score = own.T.reshape(batches, fields, 4)
-    spec = spec.reshape(-1)[:ENTRIES].reshape(FIELDS, DEV_SLOTS, 2)
-    spec_score = (spec[..., 0] + spec[..., 1]).reshape(batches, fields, DEV_SLOTS)
-    return (member_grad, row_score, spec_score)
+    variables = FIELDS // BATCHES
+    step_rows = ROWS // STEPS
+    member_grad, row_score, spec_score = pl.pallas_call(
+        combine_kernel,
+        grid=(STEPS,),
+        out_shape=(
+            jax.ShapeDtypeStruct((ROWS, LON), BF16),
+            jax.ShapeDtypeStruct((BATCHES, 4, variables), F32),
+            jax.ShapeDtypeStruct((BATCHES, DEV_SLOTS, variables), F32),
+        ),
+        in_specs=[
+            pl.BlockSpec((TILES // STEPS, 16, 128), lambda i: (i, 0, 0)),
+            pl.BlockSpec((step_rows, LON), lambda i: (i, 0)),
+            pl.BlockSpec((24, 128), lambda i: (0, 0)),
+        ],
+        out_specs=(
+            pl.BlockSpec((step_rows, LON), lambda i: (i, 0)),
+            pl.BlockSpec((BATCHES, 4, variables), lambda i: (0, 0, 0)),
+            pl.BlockSpec((BATCHES, DEV_SLOTS, variables), lambda i: (0, 0, 0)),
+        ),
+        compiler_params=pltpu.CompilerParams(vmem_limit_bytes=32 * 2**20),
+    )(slopes, grad, small)
+    return (
+        member_grad.reshape(members.shape),
+        row_score.transpose(0, 2, 1),
+        spec_score.transpose(0, 2, 1),
+    )
 
 
 def solution(mesh):

time: 275 us -> 248 us (0.902); the launches traced: 269 us -> 245 us
  Pallas kernels: 258 us -> 239 us
  local copies, waits for them, and re-layouts: 10.7 us -> 5.65 us
    pallas_call x1 -> x2, Pallas kernels: 258 us -> 239 us  [the longest x1 235 us: body(): pl.pallas_call(body_kernel, out_shape=(jax.ShapeDtypeStruct((ENS * OWN, 1...]
    unnamed x3 -> x6, local copies, waits for them, and re-layouts: 5.3 us -> 5.65 us
where the time goes in v2:
time: 248 us; the launch traced here: 245 us
  Pallas kernels  239 us (96%)
  local copies, waits for them, and re-layouts  5.65 us (2%)
    pallas_call x1, Pallas kernels, body(): pl.pallas_call(body_kernel, out_shape=(jax.ShapeDtypeStruct((ENS * OWN, 1...  235 us
    unnamed x6, local copies, waits for them, and re-layouts  5.65 us

profile of v2, /device:TPU:32, one launch (start us, length us, event | category | flops | bytes accessed | tf_op | source)
XLA Modules:
  0.0 245.1 jit_solution(5529407526986062501)
XLA Ops:
  0.6 235.2 %shard_map.76 = (bf16[816,16,128]{2,1,0:T(8,128)(2,1)}, f32[1152,1440]{1,0:T(8,128)}, f32[24,128]{1,0:T(8,128)}) custom-call(bf16[1152,1440]{1,0:T(8,128)(2,1)} %bitcast.6, bf16[1152,1440]{1,0:T(8,128)(2,1)} %bitcast.7, bf16[3,6,3,2,384]{4,3,2,1,0:T(2,128)(2,1)} %tsp.1, bf16[3,512,384]{2,1,0:T(8,128)(2,1)} %leg_hbm.1, s32[3,128]{1,0:T(4,128)} %bitcast.8, ...), custom_call_target="tpu_custom_call" | custom-call | tf_op jit(solution)/shard_map/pallas_call | solution.py:761
  235.8 0.0 copy-start
  235.8 3.0 %copy-done = f32[1152,1440]{1,0:T(8,128)S(1)} copy-done((f32[1152,1440]{1,0:T(8,128)S(1)}, f32[1152,1440]{1,0:T(8,128)}, u32[]{:S(2)}) %copy-start) | copy-done | bytes 6635544
  238.8 0.0 copy-start.1
  238.8 1.9 copy-done.1
  240.8 0.0 copy-start.2
  240.8 0.7 copy-done.2
  241.5 3.6 %shard_map.77 = (bf16[1152,1440]{1,0:T(8,128)(2,1)}, f32[3,4,6]{2,1,0:T(4,128)}, f32[3,3,6]{2,1,0:T(4,128)}) custom-call(bf16[816,16,128]{2,1,0:T(8,128)(2,1)S(1)} %copy-done.1, f32[1152,1440]{1,0:T(8,128)S(1)} %copy-done, f32[24,128]{1,0:T(8,128)S(1)} %copy-done.2), custom_call_target="tpu_custom_call" | custom-call | tf_op jit(solution)/shard_map/pallas_call | solution.py:821
Async XLA Ops:
  235.8 3.0 %copy-start = (f32[1152,1440]{1,0:T(8,128)S(1)}, f32[1152,1440]{1,0:T(8,128)}, u32[]{:S(2)}) copy-start(f32[1152,1440]{1,0:T(8,128)} %get-tuple-element.10.grad) | copy-start | bytes 19906564
  238.8 1.9 copy-start.1
  240.8 0.7 copy-start.2

commit v3 on v2

--- a/solution.py
+++ b/solution.py
@@ -72,11 +72,11 @@
 
 def body_kernel(
     mem_hbm, tgt_hbm, tsp, leg_hbm, wave_rows, wnum,
-    got_d, grad_hbm, small,
-    mem, tgt, leg, tiles, own_target, got_a, stage_a, stage_d, grad, table, send, got_b1, got_b2, got_c1, got_c2,
+    got_d, grad, small,
+    mem, tgt, leg, tiles, own_target, got_a, stage_a, stage_d, table, send, got_b1, got_b2, got_c1, got_c2,
     wide, mixed, spectral, tspec, spec_sum, part, xs, ys, scores, score_sum, got_s,
     ax_send, ax_recv, dx_send, dx_recv, a_send, a_recv, d_send, d_recv, b1_send, b1_recv, b2_send, b2_recv,
-    c1_send, c1_recv, c2_send, c2_recv, s_send, s_recv, mem_sem, tgt_sem, leg_sem, grad_sem, keep_sem,
+    c1_send, c1_recv, c2_send, c2_recv, s_send, s_recv, mem_sem, tgt_sem, leg_sem, keep_sem,
 ):
     e = lax.axis_index("ens")
     q_me = lax.axis_index("lat")
@@ -305,6 +305,16 @@
         mine = pl.ds(pl.multiple_of(me * size, size), size)
         got[mine, :] = send[mine, :]
 
+    def finish_near(copy, count, peer_of, me, got, s_sem, r_sem):
+        for k in (1, count - 1, 2, count - 2):
+            copy(send, got, s_sem, r_sem, me, peer_of(k)).wait_recv()
+
+    def finish_far(copy, count, peer_of, me, got, s_sem, r_sem):
+        for k in range(3, count - 2):
+            copy(send, got, s_sem, r_sem, me, peer_of(k)).wait_recv()
+        for k in range(1, count):
+            copy(send, got, s_sem, r_sem, peer_of(k), me).wait_send()
+
     def finish(copy, count, peer_of, me, got, s_sem, r_sem):
         def wait(k, carry):
             copy(send, got, s_sem, r_sem, peer_of(k), me).wait_send()
@@ -520,8 +530,9 @@
     grid_chunk(0)
     dx_start(0)
 
+    finish_near(z_copy, ZS, z_peer, z_me, got_b2, b2_send, b2_recv)
     a_forward(1)
-    finish(z_copy, ZS, z_peer, z_me, got_b2, b2_send, b2_recv)
+    finish_far(z_copy, ZS, z_peer, z_me, got_b2, b2_send, b2_recv)
     a_forward(2)
     widen(got_b2)
     low = lax.broadcasted_iota(jnp.int32, (16, 128), 1) < 64
@@ -638,15 +649,13 @@
 
     lax.fori_loop(0, COLS // 48, narrow, 0)
     exchange(z_copy, ZS, z_peer, z_me, per_z, got_c1, c1_send, c1_recv)
-    d_start(0)
     grid_chunk(1)
     dx_start(1)
-    d_start(1)
-    d_forward(0)
     grid_chunk(2)
     dx_start(2)
-    d_start(2)
-    d_forward(1)
+    finish_near(z_copy, ZS, z_peer, z_me, got_c1, c1_send, c1_recv)
+    d_start(0)
+    d_forward(0)
 
     lane = lax.broadcasted_iota(jnp.int32, (BAND, 128), 1)
     total = jnp.zeros((BAND, 128), F32)
@@ -672,8 +681,11 @@
     lax.fori_loop(1, ENS, s_start, 0)
     got_s[e] = score_sum[e // 2]
 
+    finish_far(z_copy, ZS, z_peer, z_me, got_c1, c1_send, c1_recv)
+    d_start(1)
+    d_forward(1)
+    d_start(2)
     d_forward(2)
-    finish(z_copy, ZS, z_peer, z_me, got_c1, c1_send, c1_recv)
     widen(got_c1)
 
     def regroup_c(place, carry):
@@ -709,8 +721,6 @@
         return carry
 
     lax.fori_loop(0, ROWS // 384, backward, 0)
-    grad_store = pltpu.make_async_copy(grad, grad_hbm, grad_sem)
-    grad_store.start()
 
     def s_wait(k, carry):
         s_copy(ens_peer(k), e).wait_send()
@@ -724,17 +734,13 @@
     lax.fori_loop(1, ENS, s_wait, 0)
     rows = jnp.sum(got_s[...], axis=0)
     small[pl.ds(0, 4), :] = jnp.where(lax.rem(e, 2) == 0, rows[:4], rows[4:])
-    grad_store.wait()
-
-
-def combine_kernel(got_d, grad, small, out, row_out, spec_out):
+
+
+def combine_kernel(got_d, grad, small, out_hbm, row_out, spec_out, out, out_sem):
     variables = FIELDS // BATCHES
-
-    @pl.when(pl.program_id(0) == 0)
-    def _():
-        for b in range(BATCHES):
-            row_out[b] = small[pl.ds(0, 4), pl.ds(b * variables, variables)]
-            spec_out[b] = small[pl.ds(8 + b * DEV_SLOTS, DEV_SLOTS), pl.ds(0, variables)]
+    for b in range(BATCHES):
+        row_out[b] = small[pl.ds(0, 4), pl.ds(b * variables, variables)]
+        spec_out[b] = small[pl.ds(8 + b * DEV_SLOTS, DEV_SLOTS), pl.ds(0, variables)]
 
     def combine(field, carry):
         top = pl.multiple_of(field * BAND, BAND)
@@ -750,7 +756,14 @@
             out[rows, lanes] = (grad[rows, lanes] + moved[:, :TAIL]).astype(BF16)
         return carry
 
-    lax.fori_loop(0, FIELDS // STEPS, combine, 0)
+    stores = []
+    for step in range(STEPS):
+        lax.fori_loop(step * (FIELDS // STEPS), (step + 1) * (FIELDS // STEPS), combine, 0)
+        rows = pl.ds(step * (ROWS // STEPS), ROWS // STEPS)
+        stores.append(pltpu.make_async_copy(out.at[rows], out_hbm.at[rows], out_sem.at[step]))
+        stores[-1].start()
+    for store in stores:
+        store.wait()
 
 
 def body(members, target, target_spectrum, legendre, wavenum):
@@ -761,12 +774,12 @@
     slopes, grad, small = pl.pallas_call(
         body_kernel,
         out_shape=(
-            jax.ShapeDtypeStruct((ENS * OWN, 16, 128), BF16),
-            jax.ShapeDtypeStruct((ROWS, LON), F32),
-            jax.ShapeDtypeStruct((24, 128), F32),
+            pltpu.VMEM((ENS * OWN, 16, 128), BF16),
+            pltpu.VMEM((ROWS, LON), F32),
+            pltpu.VMEM((24, 128), F32),
         ),
         in_specs=[hbm, hbm, vmem, hbm, vmem, pl.BlockSpec(memory_space=pltpu.SMEM)],
-        out_specs=(hbm, hbm, vmem),
+        out_specs=(vmem, vmem, vmem),
         scratch_shapes=[
             pltpu.VMEM((ROWS, LON), BF16),
             pltpu.VMEM((ROWS, LON), BF16),
@@ -776,7 +789,6 @@
             pltpu.VMEM((ENS, OWN, 16, 128), BF16),
             pltpu.VMEM((ZS, OWN, 16, 128), BF16),
             pltpu.VMEM((ZS, OWN, 16, 128), BF16),
-            pltpu.VMEM((ROWS, LON), F32),
             pltpu.VMEM((COLS, LON), BF16),
             pltpu.VMEM((COLS, ROWS), BF16),
             pltpu.VMEM((COLS, ROWS), BF16),
@@ -803,10 +815,10 @@
             dma((ZS,)), dma((ZS,)),
             dma((PLANE,)), dma((PLANE,)),
             dma((ENS,)), dma((ENS,)),
-            dma((LOADS,)), dma, dma, dma, dma((chunks, 2)),
+            dma((LOADS,)), dma, dma, dma((chunks, 2)),
         ],
         compiler_params=pltpu.CompilerParams(
-            collective_id=0, has_side_effects=True, vmem_limit_bytes=60 * 2**20
+            collective_id=0, has_side_effects=True, vmem_limit_bytes=48 * 2**20
         ),
     )(
         members.reshape(ROWS, LON),
@@ -817,26 +829,17 @@
         wavenum,
     )
     variables = FIELDS // BATCHES
-    step_rows = ROWS // STEPS
     member_grad, row_score, spec_score = pl.pallas_call(
         combine_kernel,
-        grid=(STEPS,),
         out_shape=(
             jax.ShapeDtypeStruct((ROWS, LON), BF16),
             jax.ShapeDtypeStruct((BATCHES, 4, variables), F32),
             jax.ShapeDtypeStruct((BATCHES, DEV_SLOTS, variables), F32),
         ),
-        in_specs=[
-            pl.BlockSpec((TILES // STEPS, 16, 128), lambda i: (i, 0, 0)),
-            pl.BlockSpec((step_rows, LON), lambda i: (i, 0)),
-            pl.BlockSpec((24, 128), lambda i: (0, 0)),
-        ],
-        out_specs=(
-            pl.BlockSpec((step_rows, LON), lambda i: (i, 0)),
-            pl.BlockSpec((BATCHES, 4, variables), lambda i: (0, 0, 0)),
-            pl.BlockSpec((BATCHES, DEV_SLOTS, variables), lambda i: (0, 0, 0)),
-        ),
-        compiler_params=pltpu.CompilerParams(vmem_limit_bytes=32 * 2**20),
+        in_specs=[vmem, vmem, vmem],
+        out_specs=(hbm, vmem, vmem),
+        scratch_shapes=[pltpu.VMEM((ROWS, LON), BF16), dma((STEPS,))],
+        compiler_params=pltpu.CompilerParams(vmem_limit_bytes=16 * 2**20),
     )(slopes, grad, small)
     return (
         member_grad.reshape(members.shape),

time: 248 us -> 243 us (0.980); the launches traced: 245 us -> 243 us
  local copies, waits for them, and re-layouts: 5.65 us -> 0 us
  Pallas kernels: 239 us -> 242 us
    unnamed x6 -> x0, local copies, waits for them, and re-layouts: 5.65 us -> none
    pallas_call x2, Pallas kernels: 239 us -> 242 us  [the longest x1 239 us: body(): pl.pallas_call(body_kernel, out_shape=(pltpu.VMEM((ENS * OWN, 16, 128), B...]
where the time goes in v3:
time: 243 us
  Pallas kernels  242 us (100%)
    pallas_call x1, Pallas kernels, body(): pl.pallas_call(body_kernel, out_shape=(pltpu.VMEM((ENS * OWN, 16, 128), B...  239 us

profile of v3, /device:TPU:32, one launch (start us, length us, event | category | flops | bytes accessed | tf_op | source)
XLA Modules:
  0.0 242.9 jit_solution(10992672037925889366)
XLA Ops:
  0.6 239.2 %shard_map.76 = (bf16[816,16,128]{2,1,0:T(8,128)(2,1)S(1)}, f32[1152,1440]{1,0:T(8,128)S(1)}, f32[24,128]{1,0:T(8,128)S(1)}) custom-call(bf16[1152,1440]{1,0:T(8,128)(2,1)} %bitcast.6, bf16[1152,1440]{1,0:T(8,128)(2,1)} %bitcast.7, bf16[3,6,3,2,384]{4,3,2,1,0:T(2,128)(2,1)} %tsp.1, bf16[3,512,384]{2,1,0:T(8,128)(2,1)} %leg_hbm.1, s32[3,128]{1,0:T(4,128)} %bitcast.8, ...), custom_call_target="tpu_custom_call" | custom-call | tf_op jit(solution)/shard_map/pallas_call | solution.py:774
  239.8 3.1 %shard_map.77 = (bf16[1152,1440]{1,0:T(8,128)(2,1)}, f32[3,4,6]{2,1,0:T(4,128)}, f32[3,3,6]{2,1,0:T(4,128)}) custom-call(bf16[816,16,128]{2,1,0:T(8,128)(2,1)S(1)} %get-tuple-element.9.got_d, f32[1152,1440]{1,0:T(8,128)S(1)} %get-tuple-element.10.grad, f32[24,128]{1,0:T(8,128)S(1)} %get-tuple-element.11.small), custom_call_target="tpu_custom_call" | custom-call | tf_op jit(solution)/shard_map/pallas_call | solution.py:832

commit v4 on v3

--- a/solution.py
+++ b/solution.py
@@ -38,7 +38,8 @@
 TILES = FIELDS * FIELD_TILES
 OWN = -(-TILES // ENS)
 CHUNKS = ((0, 9), (9, 18), (27, 24))
-LOADS = 3
+LOADS = 6
+EARLY = 4
 STEPS = 6
 ENTRIES = FIELDS * PARTS
 GROUPS = -(-ENTRIES // 8)
@@ -90,13 +91,19 @@
     g_me = q_me * XS + x_me
 
     def z_peer(k):
-        return lax.rem(z_me + k, ZS)
+        odd = lax.rem(k, 2)
+        away = odd * ((k + 1) // 2) + (1 - odd) * (ZS - k // 2)
+        return lax.rem(z_me + away * (1 - k // ZS), ZS)
 
     def plane_peer(k):
         return lax.rem(g_me + k, PLANE)
 
+    def part_of(index):
+        return index + x_me * (LOADS - 1 - 2 * index)
+
     def mem_load(index):
-        rows = pl.ds(index * (ROWS // LOADS), ROWS // LOADS)
+        top = pl.multiple_of(part_of(index) * (ROWS // LOADS), ROWS // LOADS)
+        rows = pl.ds(top, ROWS // LOADS)
         return pltpu.make_async_copy(mem_hbm.at[rows], mem.at[rows], mem_sem.at[index])
 
     tgt_load = pltpu.make_async_copy(tgt_hbm, tgt, tgt_sem)
@@ -138,9 +145,13 @@
         tiles[field * FIELD_TILES + FIELD_TILES - 1] = jnp.concatenate(tails, axis=1).astype(BF16)
         return carry
 
-    for index in range(LOADS):
+    def retile_part(index):
         mem_load(index).wait()
-        lax.fori_loop(index * (FIELDS // LOADS), (index + 1) * (FIELDS // LOADS), retile, 0)
+        first = part_of(index) * (FIELDS // LOADS)
+        lax.fori_loop(first, first + FIELDS // LOADS, retile, 0)
+
+    for index in range(EARLY):
+        retile_part(index)
     tiles[pl.ds(TILES, ENS * OWN - TILES)] = jnp.zeros((ENS * OWN - TILES, 16, 128), BF16)
 
     def ax_copy(chunk, z):
@@ -227,8 +238,9 @@
     pl.semaphore_wait(barrier, ENS - 1 + XS * (LATS - 1))
     for chunk in range(len(CHUNKS)):
         a_start(chunk)
-        if chunk == 0:
-            ax_start(0)
+    for index in range(EARLY, LOADS):
+        retile_part(index)
+    ax_start(0)
 
     def table_rows(index, carry):
         rows = pl.ds(pl.multiple_of(index * 64, 64), 64)
@@ -306,11 +318,11 @@
         got[mine, :] = send[mine, :]
 
     def finish_near(copy, count, peer_of, me, got, s_sem, r_sem):
-        for k in (1, count - 1, 2, count - 2):
+        for k in (1, 2, 3, 4):
             copy(send, got, s_sem, r_sem, me, peer_of(k)).wait_recv()
 
     def finish_far(copy, count, peer_of, me, got, s_sem, r_sem):
-        for k in range(3, count - 2):
+        for k in range(5, count):
             copy(send, got, s_sem, r_sem, me, peer_of(k)).wait_recv()
         for k in range(1, count):
             copy(send, got, s_sem, r_sem, peer_of(k), me).wait_send()
@@ -662,11 +674,16 @@
     for local in range(3):
         rows_sum = jnp.sum(scores[local], axis=1, keepdims=True) * (1.0 / LON)
         total = total + jnp.where(lane == field_first + local, rows_sum, 0.0)
-    score_sum[...] = total.reshape(LATS, 8, 128)
+    turn = lax.rem(lax.broadcasted_iota(jnp.int32, (BAND, 128), 0), 4)
+    packed = total
+    for place in range(1, 4):
+        packed = jnp.where(turn == place, pltpu.roll(total, 32 * place, 1), packed)
+    for peer in range(ENS):
+        score_sum[peer] = jnp.sum(packed[4 * peer : 4 * peer + 4], axis=0, keepdims=True)
 
     def s_copy(peer, slot):
         return pltpu.make_async_remote_copy(
-            src_ref=score_sum.at[peer // 2],
+            src_ref=score_sum.at[peer],
             dst_ref=got_s.at[slot],
             send_sem=s_send.at[peer],
             recv_sem=s_recv.at[slot],
@@ -679,7 +696,7 @@
         return carry
 
     lax.fori_loop(1, ENS, s_start, 0)
-    got_s[e] = score_sum[e // 2]
+    got_s[e] = score_sum[e]
 
     finish_far(z_copy, ZS, z_peer, z_me, got_c1, c1_send, c1_recv)
     d_start(1)
@@ -732,14 +749,15 @@
     for chunk in range(len(CHUNKS)):
         d_wait(chunk)
     lax.fori_loop(1, ENS, s_wait, 0)
-    rows = jnp.sum(got_s[...], axis=0)
-    small[pl.ds(0, 4), :] = jnp.where(lax.rem(e, 2) == 0, rows[:4], rows[4:])
+    small[pl.ds(0, 1), :] = jnp.sum(got_s[...], axis=0)
 
 
 def combine_kernel(got_d, grad, small, out_hbm, row_out, spec_out, out, out_sem):
     variables = FIELDS // BATCHES
     for b in range(BATCHES):
-        row_out[b] = small[pl.ds(0, 4), pl.ds(b * variables, variables)]
+        for row in range(4):
+            lanes = pl.ds(32 * row + b * variables, variables)
+            row_out[b, pl.ds(row, 1), :] = small[pl.ds(0, 1), lanes]
         spec_out[b] = small[pl.ds(8 + b * DEV_SLOTS, DEV_SLOTS), pl.ds(0, variables)]
 
     def combine(field, carry):
@@ -804,8 +822,8 @@
             pltpu.VMEM((ENS, 16, 128), F32),
             pltpu.VMEM((ENS, 16, 128), F32),
             pltpu.VMEM((3, BAND, 128), F32),
-            pltpu.VMEM((LATS, 8, 128), F32),
-            pltpu.VMEM((ENS, 8, 128), F32),
+            pltpu.VMEM((ENS, 1, 128), F32),
+            pltpu.VMEM((ENS, 1, 128), F32),
             dma((chunks, ZS)), dma((chunks, ZS)),
             dma((chunks, ZS)), dma((chunks, ZS)),
             dma((chunks, ENS)), dma((chunks, ENS)),

time: 243 us -> 240 us (0.988)
  Pallas kernels: 242 us -> 239 us
    pallas_call x1, Pallas kernels: 239 us -> 236 us  [body(): pl.pallas_call(body_kernel, out_shape=(pltpu.VMEM((ENS * OWN, 16, 128), B...]
where the time goes in v4:
time: 240 us
  Pallas kernels  239 us (100%)
    pallas_call x1, Pallas kernels, body(): pl.pallas_call(body_kernel, out_shape=(pltpu.VMEM((ENS * OWN, 16, 128), B...  236 us

profile of v4, /device:TPU:32, one launch (start us, length us, event | category | flops | bytes accessed | tf_op | source)
XLA Modules:
  0.0 239.9 jit_solution(8451191045291873523)
XLA Ops:
  0.6 236.2 %shard_map.76 = (bf16[816,16,128]{2,1,0:T(8,128)(2,1)S(1)}, f32[1152,1440]{1,0:T(8,128)S(1)}, f32[24,128]{1,0:T(8,128)S(1)}) custom-call(bf16[1152,1440]{1,0:T(8,128)(2,1)} %bitcast.6, bf16[1152,1440]{1,0:T(8,128)(2,1)} %bitcast.7, bf16[3,6,3,2,384]{4,3,2,1,0:T(2,128)(2,1)} %tsp.1, bf16[3,512,384]{2,1,0:T(8,128)(2,1)} %leg_hbm.1, s32[3,128]{1,0:T(4,128)} %bitcast.8, ...), custom_call_target="tpu_custom_call" | custom-call | tf_op jit(solution)/shard_map/pallas_call | solution.py:792
  236.8 3.1 %shard_map.77 = (bf16[1152,1440]{1,0:T(8,128)(2,1)}, f32[3,4,6]{2,1,0:T(4,128)}, f32[3,3,6]{2,1,0:T(4,128)}) custom-call(bf16[816,16,128]{2,1,0:T(8,128)(2,1)S(1)} %get-tuple-element.9.got_d, f32[1152,1440]{1,0:T(8,128)S(1)} %get-tuple-element.10.grad, f32[24,128]{1,0:T(8,128)S(1)} %get-tuple-element.11.small), custom_call_target="tpu_custom_call" | custom-call | tf_op jit(solution)/shard_map/pallas_call | solution.py:850

commit v5 on v4

--- a/solution.py
+++ b/solution.py
@@ -40,7 +40,7 @@
 CHUNKS = ((0, 9), (9, 18), (27, 24))
 LOADS = 6
 EARLY = 4
-STEPS = 6
+STEPS = 18
 ENTRIES = FIELDS * PARTS
 GROUPS = -(-ENTRIES // 8)
 
@@ -518,9 +518,12 @@
         d_cross(chunk).start()
 
     def d_wait(chunk):
-        def step(k, carry):
+        def step_send(k, carry):
             d_copy(chunk, z_peer(k), e).wait_send()
             d_pass(chunk, z_peer(k), partner).wait_send()
+            return carry
+
+        def step(k, carry):
             d_copy(chunk, z_me, x_me * ZS + z_peer(k)).wait_recv()
             d_pass(chunk, z_me, (1 - x_me) * ZS + z_peer(k)).wait_recv()
             return carry
@@ -529,10 +532,11 @@
             dx_copy(chunk, z).wait_send()
             return carry
 
-        lax.fori_loop(1, ZS, step, 0)
         lax.fori_loop(0, ZS, step_x, 0)
         d_keep(chunk).wait()
         d_cross(chunk).wait()
+        lax.fori_loop(1, ZS, step_send, 0)
+        lax.fori_loop(1, ZS, step, 0)
 
     def grid_chunk(chunk):
         a_wait(chunk)
@@ -746,10 +750,10 @@
 
     for chunk in range(len(CHUNKS)):
         a_done(chunk)
+    lax.fori_loop(1, ENS, s_wait, 0)
+    small[pl.ds(0, 1), :] = jnp.sum(got_s[...], axis=0)
     for chunk in range(len(CHUNKS)):
         d_wait(chunk)
-    lax.fori_loop(1, ENS, s_wait, 0)
-    small[pl.ds(0, 1), :] = jnp.sum(got_s[...], axis=0)
 
 
 def combine_kernel(got_d, grad, small, out_hbm, row_out, spec_out, out, out_sem):

time: 240 us -> 239 us (level)
  no operation moved by 1% of the time
where the time goes in v5:
time: 239 us
  Pallas kernels  239 us (100%)
    pallas_call x1, Pallas kernels, body(): pl.pallas_call(body_kernel, out_shape=(pltpu.VMEM((ENS * OWN, 16, 128), B...  236 us

profile of v5, /device:TPU:32, one launch (start us, length us, event | category | flops | bytes accessed | tf_op | source)
XLA Modules:
  0.0 239.2 jit_solution(13252186493099081174)
XLA Ops:
  0.6 235.9 %shard_map.76 = (bf16[816,16,128]{2,1,0:T(8,128)(2,1)S(1)}, f32[1152,1440]{1,0:T(8,128)S(1)}, f32[24,128]{1,0:T(8,128)S(1)}) custom-call(bf16[1152,1440]{1,0:T(8,128)(2,1)} %bitcast.6, bf16[1152,1440]{1,0:T(8,128)(2,1)} %bitcast.7, bf16[3,6,3,2,384]{4,3,2,1,0:T(2,128)(2,1)} %tsp.1, bf16[3,512,384]{2,1,0:T(8,128)(2,1)} %leg_hbm.1, s32[3,128]{1,0:T(4,128)} %bitcast.8, ...), custom_call_target="tpu_custom_call" | custom-call | tf_op jit(solution)/shard_map/pallas_call | solution.py:796
  236.6 2.6 %shard_map.77 = (bf16[1152,1440]{1,0:T(8,128)(2,1)}, f32[3,4,6]{2,1,0:T(4,128)}, f32[3,3,6]{2,1,0:T(4,128)}) custom-call(bf16[816,16,128]{2,1,0:T(8,128)(2,1)S(1)} %get-tuple-element.9.got_d, f32[1152,1440]{1,0:T(8,128)S(1)} %get-tuple-element.10.grad, f32[24,128]{1,0:T(8,128)S(1)} %get-tuple-element.11.small), custom_call_target="tpu_custom_call" | custom-call | tf_op jit(solution)/shard_map/pallas_call | solution.py:854
